TPU v7x, 32 devices: a whole 2x2x4 slice. The times are simulated.
32 devices in a mesh: tm: 16 (over z, y, core), batch: 2 (over x).
Axes of the slice: x: 2, y: 2, z: 4, core: 2. Of those that a mesh axis runs over, the one named last changes fastest.
Arguments:
- block_entry_input: bfloat16 [2, 8192, 384], P('batch', 'tm'), may hold values from -90 to 90
- prelude_output: bfloat16 [2, 8192, 256], P('batch', 'tm'), may hold values from -90 to 90
- leading_block_output: bfloat16 [2, 8192, 256], P('batch', 'tm'), may hold values from -90 to 90
- lengths: int32 [2, 16], P('batch'), may hold values from 1 to 1024, 8192 in all within a row
- leading_conv_weight: bfloat16 [512, 17, 384], replicated, may hold values from -0.078125 to 0.078125
- remaining_conv_weight: bfloat16 [4, 512, 17, 512], replicated, may hold values from -0.0625 to 0.0625
- gain: float32 [5, 512], replicated, may hold values from 0.25 to 1.75
- shift: float32 [5, 512], replicated, may hold values from -3 to 3
- residual_pointwise_weight: bfloat16 [512, 896], replicated, may hold values from -0.375 to 0.375
- residual_norm_scale: float32 [3, 512], replicated, may hold values from 0.4 to 0.8
- residual_norm_bias: float32 [3, 512], replicated, may hold values from -3 to 3
- cotangent: bfloat16 [2, 8192, 512], P('batch', 'tm'), may hold values from -90 to 90
Outputs:
- block_output: bfloat16 [2, 8192, 512], P('batch', 'tm')
- grad_block_input: bfloat16 [2, 8192, 384], P('batch', 'tm')
- prelude_gradient: bfloat16 [2, 8192, 256], P('batch', 'tm')
- grad_first: bfloat16 [2, 8192, 256], P('batch', 'tm')
- grad_w_first: float32 [512, 17, 384], P('tm')
- grad_w_rest: float32 [4, 512, 17, 512], P(None, 'tm')
- grad_gain: float32 [5, 512], P(None, 'tm')
- grad_shift: float32 [4, 512], P(None, 'tm')
- grad_last_shift: float32 [512], P('tm')
- grad_res_weight: float32 [512, 896], P('tm')
- grad_res_gain: float32 [3, 512], P(None, 'tm')
- grad_res_shift: float32 [3, 512], P(None, 'tm')
Inputs may be any that keep to these rules, and one draw needn't show every extreme that they name: Each row's 16 utterance lengths sum to 8192, and the longest is exactly 1024.
All inputs are finite; a program needn't handle non-finite values.
Results may differ from a plain program's by a relative error of at most 0.023.
Values may be sent and summed in bfloat16 or wider, within the bound.
No kernel may reach another device: no remote copies, remote signals or barrier semaphores. Data moves between devices by JAX's collectives and lax.ppermute only.
A program may use at most 256 MiB of HBM per device.

v0:
```python
import functools

import jax
import jax.numpy as jnp
from jax import lax
from jax.experimental import pallas as pl
from jax.experimental.pallas import tpu as pltpu
from jax.sharding import PartitionSpec as P

norm_eps = 0.001
lane = 128
half_taps = 8
group = 8
bf16 = jnp.bfloat16
f32 = jnp.float32

row_dot = (((1,), (1,)), ((), ()))
plain_dot = (((1,), (0,)), ((), ()))
column_dot = (((0,), (0,)), ((), ()))


def in_vmem():
    return pl.BlockSpec(memory_space=pltpu.VMEM)


def in_place():
    return pl.BlockSpec(memory_space=pl.ANY)


def in_smem():
    return pl.BlockSpec(memory_space=pltpu.SMEM)


def dot(a, b, dims):
    return lax.dot_general(a, b, dims, preferred_element_type=f32)


def cols(c):
    return slice(c * lane, (c + 1) * lane)


def sigmoid(v):
    return 1.0 / (1.0 + jnp.exp(-v))


def sum_rows(v):
    return jnp.sum(v, axis=0, keepdims=True)


def moments(total, row, count, samples):
    out = []
    for c in range(count):
        mean = total[row + c : row + c + 1] * (1.0 / samples)
        spread = total[row + count + c : row + count + c + 1] * (1.0 / samples) - mean * mean
        out.append((mean, lax.rsqrt(spread + norm_eps)))
    return out


class Copies:
    def __init__(self, sems):
        self.sems, self.count = sems, 0

    def start(self, src, dst):
        copy = pltpu.make_async_copy(src, dst, self.sems.at[self.count])
        self.count += 1
        copy.start()
        return copy

    def load(self, pairs):
        return [self.start(src, dst) for src, dst in pairs]


def wait_all(copies):
    for copy in copies:
        copy.wait()


def start_weights(copies, w_ref, w_vmem, layer, order):
    made = {}
    for k in order:
        made[k] = copies.start(w_ref.at[k] if layer is None else w_ref.at[layer, k], w_vmem.at[k])
    return made


def convolve(rows, base, planes, seg_ref, w_vmem, w_copies, flip, dims, acc_ref, finish=None):
    taps = w_vmem.shape[0]
    blocks = planes.shape[0]

    def add(k, low, high):
        mask = (
            seg_ref[base + k + low : base + k + high]
            == seg_ref[base + half_taps + low : base + half_taps + high]
        )
        x = jnp.concatenate(
            [jnp.where(mask, planes[c, k + low : k + high], 0.0).astype(bf16) for c in range(blocks)],
            axis=1,
        )
        d = dot(x, w_vmem[taps - 1 - k if flip else k], dims)
        if k == 0:
            acc_ref[low:high] = d
        else:
            acc_ref[low:high] += d

    whole = taps - 4 if finish else taps
    for k in range(taps):
        w_copies[taps - 1 - k if flip else k].wait()
        if k < whole:
            add(k, 0, rows)
    if finish:
        middle = rows // 32 * 16
        for low, high in ((0, middle), (middle, rows)):
            for k in range(whole, taps):
                add(k, low, high)
            finish(low, high)


def send_sums(copies, pieces, wide_ref, snd_ref):
    tile = jnp.concatenate(pieces, axis=0)
    short = wide_ref.shape[1] - tile.shape[0]
    if short:
        tile = jnp.concatenate([tile, jnp.zeros((short, lane), f32)], axis=0)
    for d in range(wide_ref.shape[0]):
        wide_ref[d] = tile
    return copies.start(wide_ref, snd_ref)


def sums_within(values, low, high, own, totals):
    inside = slice(max(low, own.start) - low, min(high, own.stop) - low)
    for i, v in enumerate(values):
        part = sum_rows(v[inside])
        totals[i] = part if totals[i] is None else totals[i] + part


def conv_finish(copies, acc_ref, a_ref, own, totals, done):
    blocks = acc_ref.shape[1] // lane

    def finish(low, high):
        done.append(copies.start(acc_ref.at[low:high], a_ref.at[low:high]))
        values = [acc_ref[low:high, cols(c)] for c in range(blocks)]
        sums_within(values + [v * v for v in values], low, high, own, totals)

    return finish


def segment_of(position, counts_ref, end, row=0):
    number = counts_ref.shape[1]
    at = lax.broadcasted_iota(jnp.int32, (1, lane), 1)
    starts, start = jnp.full((1, lane), end + lane * lane, jnp.int32), jnp.int32(0)
    for j in range(number):
        starts = jnp.where(at == j, start, starts)
        start = start + counts_ref[row, j]
    begun = jnp.where(position >= starts, 1.0, 0.0).astype(bf16)
    inside = dot(begun, jnp.ones((lane, lane), bf16), plain_dot)
    return jnp.where(position < end, inside, -1.0)


def prepare(
    frames, end, reach,
    place_ref, counts_ref, x_ref,
    seg_ref, x_tail, x_head,
    sems,
):
    copies = Copies(sems)
    edge = x_tail.shape[0]
    first = copies.load([(x_ref.at[frames - edge :], x_tail), (x_ref.at[:edge], x_head)])
    rows = lax.broadcasted_iota(jnp.int32, seg_ref.shape, 0)
    seg_ref[...] = segment_of(place_ref[0] * frames - reach + rows, counts_ref, end)
    wait_all(first)


def pack_sides(frames, p_ref, l_ref, cot_ref, s_tail, s_head, sems):
    copies = Copies(sems)
    side = s_tail.shape[0]
    at, made = 0, []
    for ref in (p_ref, l_ref, cot_ref):
        width = ref.shape[1]
        made.append(copies.start(ref.at[frames - side :], s_tail.at[:, at : at + width]))
        made.append(copies.start(ref.at[:side], s_head.at[:, at : at + width]))
        at += width
    wait_all(made)


def chunk_segments(frames, end, chunks, place_ref, counts_ref, out_ref):
    ahead = lax.broadcasted_iota(jnp.int32, out_ref.shape[1:], 0) - half_taps
    for r in range(chunks):
        row = place_ref[1, r]
        out_ref[r] = segment_of(place_ref[0, r] * frames + ahead, counts_ref, end, row).astype(bf16)


def forward_first(
    frames, ext, base,
    x_ref, low_ref, high_ref, seg_hbm, w_ref,
    a_ref, snd_ref,
    x_v, planes, seg_ref, w_vmem, acc_ref, wide_ref, sems,
):
    copies = Copies(sems)
    taps = w_vmem.shape[0]
    edge = low_ref.shape[0]
    first = copies.load([
        (x_ref, x_v.at[edge : edge + frames]), (low_ref, x_v.at[:edge]), (high_ref, x_v.at[edge + frames :]),
        (seg_hbm, seg_ref),
    ])
    w_copies = start_weights(copies, w_ref, w_vmem, None, range(taps))
    wait_all(first)
    for c in range(planes.shape[0]):
        planes[c] = x_v[:, cols(c)].astype(f32)
    done, totals = [], [None] * (2 * acc_ref.shape[1] // lane)
    finish = conv_finish(copies, acc_ref, a_ref, slice(ext, ext + frames), totals, done)
    convolve(acc_ref.shape[0], base, planes, seg_ref, w_vmem, w_copies, False, row_dot, acc_ref, finish)
    wait_all(done + [send_sums(copies, totals, wide_ref, snd_ref)])


def forward_next(
    frames, ext, base, samples, layer, with_extra,
    prev_hbm, st_hbm, gain_hbm, shift_hbm, seg_hbm, w_ref, *rest,
):
    extra_hbm, rest = (rest[0], rest[1:]) if with_extra else (None, rest)
    a_ref, h_ref, snd_ref, gain_ref, shift_ref, prev_ref, st_ref, low_ref, planes = rest[:9]
    seg_ref, w_vmem, acc_ref, wide_ref, sems = rest[9:14]
    copies = Copies(sems)
    blocks = planes.shape[0]
    small = copies.load([(st_hbm, st_ref), (gain_hbm, gain_ref), (shift_hbm, shift_ref)])
    prev_copies = [copies.start(prev_hbm.at[:, cols(c)], prev_ref.at[:, cols(c)]) for c in range(blocks)]
    seg_copy = copies.start(seg_hbm, seg_ref)
    w_copies = start_weights(copies, w_ref, w_vmem, layer - 2, range(w_vmem.shape[0]))
    extra = None
    if with_extra:
        extra = copies.start(extra_hbm.at[layer - 2], rest[14])
    wait_all(small)
    total = jnp.sum(st_ref[...], axis=0)
    inner = slice(ext + half_taps, ext + half_taps + frames)
    prev = slice(layer - 2, layer - 1)
    for c, (mean, rstd) in enumerate(moments(total, 0, blocks, samples)):
        prev_copies[c].wait()
        z = (prev_ref[:, cols(c)] - mean) * (rstd * gain_ref[prev, cols(c)])
        z = z + shift_ref[prev, cols(c)]
        low = (z * sigmoid(z)).astype(bf16)
        planes[c] = low.astype(f32)
        low_ref[:, cols(c)] = low[inner]
    h_copy = copies.start(low_ref, h_ref)
    seg_copy.wait()
    done, totals = [h_copy], [None] * (2 * blocks)
    finish = conv_finish(copies, acc_ref, a_ref, slice(ext, ext + frames), totals, done)
    convolve(acc_ref.shape[0], base, planes, seg_ref, w_vmem, w_copies, False, row_dot, acc_ref, finish)
    if with_extra:
        extra.wait()
        totals.append(rest[14][...])
    wait_all(done + [send_sums(copies, totals, wide_ref, snd_ref)])


def branch_weights(rw_ref, sources):
    at, out = 0, []
    for p in sources:
        out.append(rw_ref[:, at : at + p.shape[1]])
        at += p.shape[1]
    return out


def branch_sums(p_ref, l_ref, x_ref, rw_ref, out_ref):
    blocks = rw_ref.shape[0] // lane
    sources = (p_ref, l_ref, x_ref)
    for branch, (p, w) in enumerate(zip(sources, branch_weights(rw_ref, sources), strict=True)):
        q = dot(p[...], w, row_dot)
        for c in range(blocks):
            out_ref[branch, c : c + 1] = sum_rows(q[:, cols(c)])
            out_ref[branch, blocks + c : blocks + c + 1] = sum_rows(q[:, cols(c)] * q[:, cols(c)])


def join(
    frames, ext, samples, layer,
    a_hbm, st_hbm, p_hbm, l_hbm, x_hbm, rw_hbm, q0_hbm, q1_hbm, q2_hbm, cot_hbm, xl_hbm, xh_hbm, sl_hbm, sh_hbm,
    gain_ref, shift_ref, rg_ref, rb_ref,
    out_ref, du_ref, snd_ref, snd_res_ref, q_tot_ref,
    a_ref, st_ref, p_ref, l_ref, x_ref, rw_ref, qst_refs, cot_ref, x_low, x_high, s_low, s_high,
    q_ref, du_v, out_v, wide_ref, wide_res_ref, sems,
):
    copies = Copies(sems)
    blocks = a_ref.shape[1] // lane
    early = copies.load([
        (rw_hbm, rw_ref), (p_hbm, p_ref), (l_hbm, l_ref), (x_hbm, x_ref), (xl_hbm, x_low), (xh_hbm, x_high),
        (sl_hbm, s_low), (sh_hbm, s_high),
    ])
    first = copies.load(
        [(q, qst_refs.at[i]) for i, q in enumerate((q0_hbm, q1_hbm, q2_hbm))] + [(st_hbm, st_ref)]
    )
    columns = [
        copies.load([
            (a_hbm.at[:, cols(c)], a_ref.at[:, cols(c)]), (cot_hbm.at[:, cols(c)], cot_ref.at[:, cols(c)]),
        ])
        for c in range(blocks)
    ]
    wait_all(early)
    sources = (p_ref, l_ref, x_ref)
    edge, side = x_low.shape[0], s_low.shape[0]
    own = slice(ext, ext + frames)
    at = 0
    for branch, w in enumerate(branch_weights(rw_ref, sources)):
        width = sources[branch].shape[1]
        if branch < 2:
            low, high = s_low[:, at : at + width], s_high[:, at : at + width]
            at += width
        else:
            low, high = x_low[edge - side :], x_high[:side]
        q_ref[branch, :ext] = dot(low, w, row_dot)[side - ext :]
        q_ref[branch, own] = dot(sources[branch][...], w, row_dot)
        q_ref[branch, ext + frames :] = dot(high, w, row_dot)[:ext]
    wait_all(first)
    total = jnp.sum(st_ref[...], axis=0)
    main = moments(total, 0, blocks, samples)
    res = []
    for branch in range(3):
        q_tot_ref[branch] = jnp.sum(qst_refs[branch], axis=0)[2 * blocks :]
        res.append(moments(q_tot_ref[branch], 0, blocks, samples))
    shift_sums, gain_sums, res_sums, done = [], [], [[], [], []], []
    mine = slice(layer - 1, layer)
    for c in range(blocks):
        wait_all(columns[c])
        normed = (a_ref[:, cols(c)] - main[c][0]) * main[c][1]
        u = normed * gain_ref[mine, cols(c)] + shift_ref[mine, cols(c)]
        normed_q = []
        for branch in range(3):
            mean, rstd = res[branch][c]
            qn = (q_ref[branch, :, cols(c)] - mean) * rstd
            normed_q.append(qn[own])
            u = u + qn * rg_ref[branch : branch + 1, cols(c)] + rb_ref[branch : branch + 1, cols(c)]
        s = sigmoid(u)
        out_v[:, cols(c)] = (u * s)[own].astype(bf16)
        slope = s * (1.0 + u * (1.0 - s))
        cot = slice(at + c * lane, at + (c + 1) * lane)
        du_v[:ext, cols(c)] = s_low[:, cot].astype(f32)[side - ext :] * slope[:ext]
        du_v[ext + frames :, cols(c)] = s_high[:, cot].astype(f32)[:ext] * slope[ext + frames :]
        du = cot_ref[:, cols(c)].astype(f32) * slope[own]
        du_v[own, cols(c)] = du
        done.append(copies.start(du_v.at[:, cols(c)], du_ref.at[:, cols(c)]))
        shift_sums.append(sum_rows(du))
        gain_sums.append(sum_rows(du * normed[own]))
        for branch in range(3):
            res_sums[branch].append(sum_rows(du * normed_q[branch]))
    done.append(copies.start(out_v, out_ref))
    done.append(send_sums(copies, shift_sums + gain_sums, wide_ref, snd_ref))
    done.append(send_sums(copies, res_sums[0] + res_sums[1] + res_sums[2], wide_res_ref, snd_res_ref))
    wait_all(done)


def branch_grads(
    frames, ext, samples,
    du_ref, bst_ref, rst_ref, p_ref, l_ref, x_ref, rw_ref, qst_ref, rg_ref,
    g0_ref, g1_ref, g2_ref, gw_ref, tot_ref,
):
    blocks = rw_ref.shape[0] // lane
    total = jnp.sum(bst_ref[...], axis=0) * (1.0 / samples)
    gains = jnp.sum(rst_ref[...], axis=0)
    tot_ref[...] = gains
    gains = gains * (1.0 / samples)
    own = slice(ext, ext + frames)
    sources = (p_ref, l_ref, x_ref)
    at_col = 0
    for branch, (g_ref, w) in enumerate(
        zip((g0_ref, g1_ref, g2_ref), branch_weights(rw_ref, sources), strict=True)
    ):
        p = sources[branch][...]
        q = dot(p, w, row_dot)
        low = []
        for c, (mean, rstd) in enumerate(moments(qst_ref[branch], 0, blocks, samples)):
            at = branch * blocks + c
            qn = (q[:, cols(c)] - mean) * rstd
            v = du_ref[own, cols(c)] - total[c : c + 1] - qn * gains[at : at + 1]
            low.append((v * (rg_ref[branch : branch + 1, cols(c)] * rstd)).astype(bf16))
        low = jnp.concatenate(low, axis=1)
        g_ref[...] = dot(low, w, plain_dot).astype(g_ref.dtype)
        width = p.shape[1]
        gw_ref[:, at_col : at_col + width] = dot(low, p, column_dot).astype(bf16)
        at_col += width


def channel_order(channels, peers, unit):
    per = channels // peers
    n = lax.broadcasted_iota(jnp.int32, (1, channels), 1)
    source = (n % per // unit * peers + n // per) * unit + n % unit
    row = lax.broadcasted_iota(jnp.int32, (channels, channels), 0)
    return jnp.where(row == source, 1.0, 0.0).astype(bf16)


def lane_group(per):
    return lax.broadcasted_iota(jnp.int32, (1, lane), 1) // per


def turn(v, lanes):
    return pltpu.roll(v, lanes % lane, 1) if lanes % lane else v


def pick_lanes(which, parts):
    out = parts[0]
    for j in range(1, len(parts)):
        out = jnp.where(which == j, parts[j], out)
    return out


class InputGrad:
    def __init__(self, copies, bst_hbm, st_hbm, dz_hbm, a_hbm, bst_v, st_v, dz_v, a_v, off_a):
        rows, channels = dz_v.shape
        self.blocks = channels // lane
        self.bst_v, self.st_v, self.dz_v, self.a_v = bst_v, st_v, dz_v, a_v
        self.first = copies.load([(bst_hbm, bst_v), (st_hbm, st_v)])
        self.columns = [
            copies.load([
                (dz_hbm.at[:, cols(c)], dz_v.at[:, cols(c)]),
                (a_hbm.at[off_a : off_a + rows, cols(c)], a_v.at[:, cols(c)]),
            ])
            for c in range(self.blocks)
        ]

    def make(self, samples, gain_row, tot_ref, at, low_ref, put):
        blocks = self.blocks
        wait_all(self.first)
        sums = jnp.sum(self.bst_v[...], axis=0)
        tot_ref[...] = sums
        sums = sums * (1.0 / samples)
        total = jnp.sum(self.st_v[...], axis=0)
        near = low_ref.shape[0]
        for c, (mean, rstd) in enumerate(moments(total, 0, blocks, samples)):
            wait_all(self.columns[c])
            normed = (self.a_v[:, cols(c)] - mean) * rstd
            v = self.dz_v[:, cols(c)] - sums[c : c + 1] - normed * sums[blocks + c : blocks + c + 1]
            low = (v * (gain_row[:, cols(c)] * rstd)).astype(bf16)
            put(c, low)
            low_ref[:, cols(c)] = low.astype(f32)[at : at + near].astype(bf16)


def pack_peers(frames, unit, low_ref, xs_ref):
    channels = low_ref.shape[1]
    peers, held = xs_ref.shape[:2]
    per = channels // peers
    fold = lane // per
    step = frames // fold
    which = lane_group(per)
    ordered = dot(low_ref[...], channel_order(channels, peers, unit), plain_dot)
    for c in range(channels // lane):
        v = ordered[:, cols(c)]
        turned = [turn(v, i * per) for i in range(fold)]
        for i in range(fold):
            parts = [turned[(j - i) % fold][j * step : j * step + held] for j in range(fold)]
            xs_ref[fold * c + i] = pick_lanes(which, parts).astype(bf16)


def backward_step(
    frames, ext_da, off_a, off_prev, base, samples, layer, unit,
    dz_hbm, bst_hbm, a_hbm, st_hbm, gain_hbm, shift_hbm, seg_hbm, w_ref, prev_hbm, prev_st_hbm,
    out_ref, x_ref, tot_ref, snd_ref,
    gain_ref, shift_ref, dz_v, bst_v, a_v, st_v, seg_ref, prev_v, prev_st_v, planes, low_ref, xs_ref, w_vmem, acc_ref, out_v, wide_ref,
    sems,
):
    copies = Copies(sems)
    affine = copies.load([(gain_hbm, gain_ref), (shift_hbm, shift_ref)])
    grad = InputGrad(copies, bst_hbm, st_hbm, dz_hbm, a_hbm, bst_v, st_v, dz_v, a_v, off_a)
    rows, channels = dz_v.shape
    blocks = channels // lane
    seg_copy = copies.start(seg_hbm, seg_ref)
    w_copies = start_weights(copies, w_ref, w_vmem, layer - 2, range(w_vmem.shape[0] - 1, -1, -1))
    out_rows = rows - 2 * half_taps
    late = copies.load([
        (prev_hbm.at[off_prev : off_prev + out_rows], prev_v), (prev_st_hbm, prev_st_v),
    ])

    def put(c, low):
        planes[c] = low.astype(f32)

    at = ext_da - half_taps
    wait_all(affine)
    grad.make(samples, gain_ref[layer - 1 : layer], tot_ref, at, low_ref, put)
    pack_peers(frames, unit, low_ref, xs_ref)
    x_copy = copies.start(xs_ref, x_ref)
    seg_copy.wait()
    own = slice(at, at + frames)
    done, totals = [x_copy], [None] * (2 * blocks)
    before = slice(layer - 2, layer - 1)

    def finish(low, high):
        if low == 0:
            wait_all(late)
        prev_moments = moments(jnp.sum(prev_st_v[...], axis=0), 0, blocks, samples)
        values, products = [], []
        for c, (mean, rstd) in enumerate(prev_moments):
            normed = (prev_v[low:high, cols(c)] - mean) * rstd
            z = normed * gain_ref[before, cols(c)] + shift_ref[before, cols(c)]
            s = sigmoid(z)
            dz = acc_ref[low:high, cols(c)] * (s * (1.0 + z * (1.0 - s)))
            out_v[low:high, cols(c)] = dz
            values.append(dz)
            products.append(dz * normed)
        done.append(copies.start(out_v.at[low:high], out_ref.at[low:high]))
        sums_within(values + products, low, high, own, totals)

    convolve(
        out_rows, base, planes, seg_ref, w_vmem, w_copies, True, plain_dot, acc_ref, finish
    )
    done.append(send_sums(copies, totals, wide_ref, snd_ref))
    wait_all(done)


def backward_norm(
    frames, ext_da, off_a, samples, layer, unit,
    dz_hbm, bst_hbm, a_hbm, st_hbm, gain_hbm,
    da_ref, x_ref, tot_ref,
    gain_ref, dz_v, bst_v, a_v, st_v, da_v, low_ref, xs_ref, sems,
):
    copies = Copies(sems)
    affine = copies.start(gain_hbm, gain_ref)
    grad = InputGrad(copies, bst_hbm, st_hbm, dz_hbm, a_hbm, bst_v, st_v, dz_v, a_v, off_a)
    affine.wait()

    def put(c, low):
        da_v[:, cols(c)] = low

    grad.make(samples, gain_ref[layer - 1 : layer], tot_ref, ext_da - half_taps, low_ref, put)
    pack_peers(frames, unit, low_ref, xs_ref)
    wait_all(copies.load([(xs_ref, x_ref), (da_v, da_ref)]))


def backward_conv(
    base, da_hbm, seg_hbm, w_ref, add_hbm, out_ref,
    da_v, seg_ref, add_v, planes, w_vmem, acc_ref, out_v, sems,
):
    copies = Copies(sems)
    first = copies.load([(da_hbm, da_v), (seg_hbm, seg_ref)])
    w_copies = start_weights(copies, w_ref, w_vmem, None, range(w_vmem.shape[0] - 1, -1, -1))
    late = copies.start(add_hbm, add_v)
    wait_all(first)
    for c in range(planes.shape[0]):
        planes[c] = da_v[:, cols(c)].astype(f32)
    convolve(acc_ref.shape[0], base, planes, seg_ref, w_vmem, w_copies, True, plain_dot, acc_ref)
    late.wait()
    out_v[...] = (acc_ref[...] + add_v[...]).astype(out_v.dtype)
    copies.start(out_v, out_ref).wait()


def weight_grads(
    frames, taps, unit,
    x_ref, segs_ref, h_ref, out_ref,
    acc_ref, x_v, seg_v, h_v, folded, stacked, seg_f, seg_stacked, out_v, sems,
):
    copies = Copies(sems)
    peers, held = x_ref.shape[:2]
    slots = out_ref.shape[0]
    per = slots * unit
    fold = lane // per
    step = frames // fold
    near = frames + 2 * half_taps
    chunk = [
        copies.load([(x_ref.at[r], x_v.at[r]), (segs_ref.at[r], seg_v.at[r]), (h_ref.at[r], h_v.at[r])])
        for r in range(peers)
    ]
    which = lane_group(per)
    pieces, done = -(-taps // fold), []
    edges = [0] + [q * step + half_taps for q in range(1, fold)] + [near]
    for r in range(peers):
        b = r % 2
        wait_all(chunk[r][:2])
        v = x_v[r].astype(f32)
        for i in range(fold):
            folded[b, i, :held] = turn(v, i * per)
        for q in range(fold):
            lo, hi = edges[q], edges[q + 1]
            at = lo - q * step
            stacked[b, lo:hi] = pick_lanes(
                which,
                [folded[b, (j - q) % fold, at + j : at + j + hi - lo] for j in range(fold)],
            )
        seg_f[b, :near] = seg_v[r].astype(f32)
        seg_stacked[b] = pick_lanes(which, [seg_f[b, j : j + near] for j in range(fold)])
        chunk[r][2].wait()
        for p in range(0, pieces, 3):
            q = min(pieces, p + 3)
            parts = [
                jnp.where(
                    seg_stacked[b, fold * n : fold * n + frames] == seg_f[b, half_taps : half_taps + frames],
                    stacked[b, fold * n : fold * n + frames],
                    0.0,
                ).astype(bf16)
                for n in range(p, q)
            ]
            d = dot(jnp.concatenate(parts, axis=1), h_v[r], column_dot)
            if r == 0:
                acc_ref[p * lane : q * lane] = d
            elif r < peers - 1:
                acc_ref[p * lane : q * lane] += d
            else:
                d = acc_ref[p * lane : q * lane] + d
                low, high = max(0, taps - q * fold), taps - p * fold
                for k in range(low, high):
                    at = (taps - 1 - k - p * fold) * per
                    for n in range(slots):
                        out_v[n, k] = d[at + n * unit : at + (n + 1) * unit].astype(bf16)
                done.append(copies.start(out_v.at[:, low:high], out_ref.at[:, low:high]))
    wait_all(done)


def call(body, name, out_shape, in_specs, scratch, flops, byte_count, args, out_specs=None, budget=60):
    out_specs = out_specs or jax.tree.map(lambda _: in_vmem(), out_shape)
    return pl.pallas_call(
        body,
        out_shape=out_shape,
        in_specs=in_specs,
        out_specs=out_specs,
        scratch_shapes=scratch,
        compiler_params=pltpu.CompilerParams(vmem_limit_bytes=budget << 20),
        cost_estimate=pl.CostEstimate(flops=flops, bytes_accessed=byte_count, transcendentals=0),
        name=name,
    )(*args)


def after(value, *others):
    return lax.optimization_barrier((value, *others))[0]


def per_device(
    block_entry_input,
    prelude_output,
    leading_block_output,
    lengths,
    leading_conv_weight,
    remaining_conv_weight,
    gain,
    shift,
    residual_pointwise_weight,
    residual_norm_scale,
    residual_norm_bias,
    cotangent,
):
    tm, rows_axis = lax.axis_size("tm"), lax.axis_size("batch")
    everyone = ("tm", "batch")
    devices = tm * rows_axis
    place = lax.axis_index("tm")
    frames, entry_width = block_entry_input.shape[1:]
    channels, taps = leading_conv_weight.shape[:2]
    blocks = channels // lane
    layers = remaining_conv_weight.shape[0] + 1
    samples = float(frames * tm * rows_axis)
    end = frames * tm
    reach = half_taps * 2 * layers
    ext = [reach - half_taps * i for i in range(layers + 1)]
    ext_u = ext[layers]
    side = -(-ext_u // 16) * 16
    unit = channels // tm
    group_count = devices // group
    groups = [[j * group + i for i in range(group)] for j in range(group_count)]
    across = [[j * group + i for j in range(group_count)] for i in range(group)]
    row_place = lax.axis_index("batch")
    me = place * rows_axis + row_place
    share_rows = channels // devices
    near = frames + 2 * half_taps

    def sds(shape, dtype):
        return jax.ShapeDtypeStruct(shape, dtype)

    def swap(v, axis, bit):
        n = lax.axis_size(axis)
        return lax.ppermute(v, axis, [(i, i ^ bit) for i in range(n)])

    def spread(v):
        return lax.all_to_all(v, everyone, 0, 0, tiled=True)

    x_own, p_own, l_own = block_entry_input[0], prelude_output[0], leading_block_output[0]
    cot_own = cotangent[0]
    side_width = p_own.shape[1] + l_own.shape[1] + channels
    place_1 = place.astype(jnp.int32).reshape(1)

    any_ = in_place
    vmem, smem = in_vmem, in_smem

    def sems(count):
        return pltpu.SemaphoreType.DMA((count,))

    seg, x_tail, x_head = call(
        functools.partial(prepare, frames, end, reach), "prepare",
        (
            sds((frames + 2 * reach, lane), f32),
            sds((reach, entry_width), bf16), sds((reach, entry_width), bf16),
        ),
        [smem()] * 2 + [any_()], [sems(2)], 1000, 1 << 20, (place_1, lengths, x_own),
    )
    upward = [(i, i + 1) for i in range(tm - 1)]
    downward = [(i + 1, i) for i in range(tm - 1)]
    x_low, x_high = lax.ppermute(x_tail, "tm", upward), lax.ppermute(x_head, "tm", downward)

    members = (me // group * group + jnp.arange(group)).astype(jnp.int32)
    group_places = jnp.stack([members // rows_axis, members % rows_axis])
    if rows_axis == 2:
        other_lengths = swap(after(lengths, x_low, x_high), "batch", 1)
        mine = jnp.where(row_place == 0, lengths, other_lengths)
        all_lengths = jnp.concatenate([mine, lengths + other_lengths - mine], axis=0)
    else:
        all_lengths = lax.all_gather(lengths[0], "batch")

    w_first = jnp.transpose(leading_conv_weight, (1, 0, 2))
    w_rest = jnp.transpose(remaining_conv_weight, (0, 2, 1, 3))

    def weights(layer):
        return (w_first, entry_width) if layer == 1 else (w_rest, channels)

    tile_sums = sds((devices, 2 * blocks, lane), f32)
    res_rows = -(-3 * blocks // 8) * 8
    sums_v = pltpu.VMEM(tile_sums.shape, f32)
    affine_v = [pltpu.VMEM(gain.shape, f32), pltpu.VMEM(shift.shape, f32)]
    seg_rows = pltpu.VMEM((frames + 2 * reach, lane), f32)

    def conv_cost(rows, width):
        return 2 * rows * width * channels * taps, 2 * taps * width * channels + 8 * rows * channels

    def planes(rows, width):
        return pltpu.VMEM((width // lane, rows, lane), f32)

    def wide_rows(rows, width, dtype=f32):
        return pltpu.VMEM((rows, width), dtype)

    def segments(chunk_places, counts):
        chunks = chunk_places.shape[1]
        return call(
            functools.partial(chunk_segments, frames, end, chunks), "chunk_segments",
            sds((chunks, near, lane), bf16), [smem()] * 2, [], 1000, 4 << 20, (chunk_places, counts),
        )

    segs = segments(group_places, all_lengths)
    row_count = [frames + 2 * e for e in ext]
    a, snd = call(
        functools.partial(forward_first, frames, ext[1], reach - ext[0]), "forward_first",
        (sds((row_count[1], channels), f32), tile_sums),
        [any_()] * 5,
        [
            wide_rows(row_count[0], entry_width, bf16), planes(row_count[0], entry_width), seg_rows,
            pltpu.VMEM((taps, channels, entry_width), bf16), wide_rows(row_count[1], channels), sums_v,
            sems(taps + 7),
        ],
        *conv_cost(row_count[1], entry_width), (x_own, x_low, x_high, seg, w_first),
        (any_(), any_()),
    )
    stats, acts = [None, spread(snd)], [None, a]
    gathered = []

    def gather(h):
        gathered.append(lax.all_gather(h, everyone, axis=0, axis_index_groups=groups))

    gather(x_own)
    q_sums = call(
        branch_sums, "branch_sums", sds((3, 2 * blocks, lane), f32),
        [vmem()] * 4, [], 2 * frames * residual_pointwise_weight.size, 4 << 20,
        (p_own, l_own, x_own, residual_pointwise_weight),
    )
    s_tail, s_head = call(
        functools.partial(pack_sides, frames), "pack_sides",
        (sds((side, side_width), bf16), sds((side, side_width), bf16)),
        [any_()] * 3, [sems(6)], 1000, 1 << 20, (p_own, l_own, cot_own),
    )
    s_low, s_high = lax.ppermute(s_tail, "tm", upward), lax.ppermute(s_head, "tm", downward)
    for layer in range(2, layers + 1):
        held = []
        if layer == 2:
            held = [s_tail, q_sums, segs]
        if layer == 5:
            held = [s_low, s_high, gathered[0]]
        if held:
            stats[layer - 1] = after(stats[layer - 1], *held)
        rows, before = row_count[layer], row_count[layer - 1]
        st = stats[layer - 1]
        with_extra = layer <= 4
        tile = sds((devices, 4 * blocks, lane), f32) if with_extra else tile_sums
        a, h, snd = call(
            functools.partial(
                forward_next, frames, ext[layer], reach - ext[layer - 1], samples, layer, with_extra
            ),
            "forward_next",
            (sds((rows, channels), f32), sds((frames, channels), bf16), tile),
            [any_()] * (6 + with_extra),
            [
                *affine_v, wide_rows(before, channels), pltpu.VMEM(st.shape, f32), wide_rows(frames, channels, bf16),
                planes(before, channels), seg_rows, pltpu.VMEM((taps, channels, channels), bf16),
                wide_rows(rows, channels), pltpu.VMEM(tile.shape, f32), sems(taps + blocks + 9),
                *([pltpu.VMEM((2 * blocks, lane), f32)] if with_extra else []),
            ],
            *conv_cost(rows, channels),
            (acts[-1], st, gain, shift, seg, w_rest, *([q_sums] if with_extra else [])),
            (any_(), any_(), any_()),
        )
        stats.append(spread(snd))
        acts.append(a)
        gather(after(h, stats[layer]))

    rows = row_count[layers]
    rw = residual_pointwise_weight

    def like(v):
        return pltpu.VMEM(v.shape, v.dtype)

    block_output, du, snd, res_snd, q_tot = call(
        functools.partial(join, frames, ext_u, samples, layers), "join",
        (
            sds((frames, channels), bf16), sds((rows, channels), f32), tile_sums,
            sds((devices, res_rows, lane), f32), sds((3, 2 * blocks, lane), f32),
        ),
        [any_()] * 14 + [vmem()] * 4,
        [
            like(acts[layers]), like(stats[layers]), like(p_own), like(l_own), like(x_own), like(rw),
            pltpu.VMEM((3, *stats[2].shape), f32), like(cot_own), like(x_low), like(x_high), like(s_low),
            like(s_high),
            pltpu.VMEM((3, rows, channels), f32), wide_rows(rows, channels),
            wide_rows(frames, channels, bf16), sums_v, pltpu.VMEM((devices, res_rows, lane), f32),
            sems(3 * blocks + 15),
        ],
        2 * rows * rw.size, 8 << 20,
        (
            acts[layers], after(stats[layers], gathered[1]), p_own, l_own, x_own, rw, *stats[2:5],
            cot_own, x_low, x_high, s_low, s_high, gain, shift, residual_norm_scale, residual_norm_bias,
        ),
        (any_(), any_(), any_(), any_(), vmem()),
    )
    back = [None] * (layers + 1)
    back[layers] = spread(snd)
    res_back = spread(res_snd)

    prelude_gradient, grad_first, res_entry, res_weight, res_tot = call(
        functools.partial(branch_grads, frames, ext_u, samples), "branch_grads",
        (
            sds(p_own.shape, bf16), sds(l_own.shape, bf16), sds(x_own.shape, f32),
            sds(residual_pointwise_weight.shape, bf16), sds((res_rows, lane), f32),
        ),
        [vmem()] * 9, [], 6 * frames * residual_pointwise_weight.size, 8 << 20,
        (
            du, back[layers], res_back, p_own, l_own, x_own, residual_pointwise_weight, q_tot,
            residual_norm_scale,
        ),
    )
    grads, totals = [None] * (layers + 1), [None] * (layers + 1)
    xs, turned, made, sent, sums = {}, {}, {}, {}, {}

    def exchange(x):
        return lax.all_to_all(x, everyone, 0, 0, tiled=True, axis_index_groups=groups)

    x_sds = sds((group, frames * channels // group // lane + 2 * half_taps, lane), bf16)
    x_v = pltpu.VMEM(x_sds.shape, bf16)

    def make_grad(layer, x):
        width = gathered[layer - 1].shape[2]
        peers, held = x.shape[:2]
        per = channels // peers
        fold = lane // per
        rows = 16
        out = (per // rows, taps, rows, width)
        return call(
            functools.partial(weight_grads, frames, taps, rows), "weight_grads", sds(out, bf16),
            [any_()] * 3,
            [
                wide_rows(-(-taps // fold) * lane, width), pltpu.VMEM(x.shape, bf16),
                pltpu.VMEM((peers, near, lane), bf16), pltpu.VMEM((peers, frames, width), bf16),
                pltpu.VMEM((2, fold, held + 8, lane), f32), pltpu.VMEM((2, near, lane), f32),
                pltpu.VMEM((2, near + 8, lane), f32), pltpu.VMEM((2, near, lane), f32),
                pltpu.VMEM(out, bf16), sems(3 * peers + (taps + 2) // 3),
            ],
            2 * taps * per * frames * peers * width, 2 * peers * frames * width,
            (x, segs, gathered[layer - 1]), any_(),
        )

    def reduce_groups(part):
        parts, rows = part.shape[0], part.shape[2]
        split = rows // share_rows
        if split > 1:
            part = part.reshape(parts, taps, split, share_rows, -1).transpose(0, 2, 1, 3, 4)
            part = part.reshape(parts * split, taps, share_rows, -1)
        return lax.psum_scatter(part, everyone, scatter_dimension=0, axis_index_groups=across)

    def halve_groups(part, late, later):
        if rows_axis != 2 or group_count != 4:
            return reduce_groups(part)
        number = me // group

        def pick(v, axis, i):
            return lax.dynamic_index_in_dim(v, i, axis, keepdims=False)

        pairs = part.reshape(2, 2, *part.shape[1:])
        away = after(swap(pick(pairs, 1, 1 - number % 2), "tm", tm // 4), late)
        both = (pick(pairs, 1, number % 2).astype(f32) + away.astype(f32)).astype(bf16)
        away = after(swap(pick(both, 0, 1 - number // 2), "tm", tm // 2), later)
        return (pick(both, 0, number // 2).astype(f32) + away.astype(f32)).astype(bf16)

    def fetch(part):
        if rows_axis == 2:
            return swap(part, "batch", 1)
        return lax.all_gather(part, "batch", axis=0)

    def added(part, other):
        if rows_axis == 2:
            return part.astype(f32) + other.astype(f32)
        return jnp.sum(other.astype(f32), axis=0)

    def joined(part, other):
        if rows_axis == 2:
            first = jnp.where(row_place == 0, part, other)
            last = jnp.where(row_place == 0, other, part)
            return jnp.concatenate([first, last], axis=1).astype(f32)
        return jnp.concatenate([other[i] for i in range(rows_axis)], axis=1).astype(f32)

    class Halving:
        def __init__(self, part):
            bits = [1 << i for i in range((tm - 1).bit_length())]
            self.order = [1, *bits[2:], 2]
            self.left, self.part = bits, part
            self.send()

        def send(self):
            bit = self.order[0]
            below = 1 << self.left.index(bit)
            self.pairs = self.part.reshape(self.part.shape[0] // below // 2, 2, below, unit, -1)
            away = lax.dynamic_index_in_dim(self.pairs, 1 - place // bit % 2, 1, keepdims=False)
            self.there = swap(away, "tm", bit)

        def step(self, *late):
            bit = self.order.pop(0)
            self.left = [b for b in self.left if b != bit]
            mine = lax.dynamic_index_in_dim(self.pairs, place // bit % 2, 1, keepdims=False)
            there = after(self.there, *late)
            part = (mine.astype(f32) + there.astype(f32)).astype(bf16)
            self.part = part.reshape(-1, unit, part.shape[-1])
            if self.order:
                self.send()

    dz = du
    for layer in range(layers, 1, -1):
        ext_da = half_taps * layer
        rows = frames + 2 * ext_da
        out_rows = rows - 2 * half_taps
        held = []
        if layer + 2 <= layers:
            made[layer + 2] = make_grad(layer + 2, after(turned[layer + 2], sent[layer]))
            held.append(made[layer + 2])
            sums[layer + 2] = reduce_groups(after(made[layer + 2], back[layer]))
        if layer == layers:
            held += [gathered[2]]
        if layer == layers - 1:
            held += [prelude_gradient]
        if layer == layers - 2:
            held += [gathered[4]]
        bst = after(back[layer], *held) if held else back[layer]
        if layer == layers - 1:
            res_part = Halving(after(res_weight, bst).reshape(tm, unit, -1))
        if layer == 2:
            res_part.step(bst)
        if layer + 1 <= layers:
            turned[layer + 1] = exchange(after(xs[layer + 1], bst))
        dz, xs[layer], totals[layer], snd = call(
            functools.partial(
                backward_step, frames, ext_da, ext[layer] - ext_da,
                ext[layer - 1] - (ext_da - half_taps), reach - ext_da, samples, layer, share_rows,
            ),
            "backward_step",
            (sds((out_rows, channels), f32), x_sds, sds((2 * blocks, lane), f32), tile_sums),
            [any_()] * 10,
            [
                *affine_v, wide_rows(rows, channels), sums_v, wide_rows(rows, channels),
                pltpu.VMEM(stats[layer].shape, f32), seg_rows,
                wide_rows(out_rows, channels), pltpu.VMEM(stats[layer - 1].shape, f32), planes(rows, channels),
                wide_rows(near, channels, bf16), x_v,
                pltpu.VMEM((taps, channels, channels), bf16), wide_rows(out_rows, channels),
                wide_rows(out_rows, channels), sums_v,
                sems(taps + 3 * blocks + 9),
            ],
            *conv_cost(out_rows, channels),
            (
                dz, bst, acts[layer], stats[layer], gain, shift, seg, w_rest, acts[layer - 1],
                stats[layer - 1],
            ),
            (any_(), any_(), vmem(), any_()),
        )
        if layer + 1 <= layers:
            snd = after(snd, turned[layer + 1])
        if layer in (layers - 1, 2):
            snd = after(snd, res_part.there)
        back[layer - 1] = spread(snd)
        sent[layer - 1] = snd

    ext_da = half_taps
    rows = frames + 2 * ext_da
    made[3] = make_grad(3, after(turned[3], sent[1]))
    sums[3] = reduce_groups(after(made[3], back[1]))
    bst = after(back[1], made[3], sums[layers])
    res_part.step(bst)
    turned[2] = exchange(after(xs[2], bst))
    da, x, totals[1] = call(
        functools.partial(backward_norm, frames, ext_da, ext[1] - ext_da, samples, 1, share_rows),
        "backward_norm",
        (sds((rows, channels), bf16), x_sds, sds((2 * blocks, lane), f32)),
        [any_()] * 5,
        [
            affine_v[0], wide_rows(rows, channels), sums_v, wide_rows(rows, channels), sums_v,
            wide_rows(rows, channels, bf16), wide_rows(near, channels, bf16),
            x_v, sems(2 * blocks + 5),
        ],
        1000, 4 << 20, (dz, bst, acts[1], stats[1], gain), (any_(), any_(), vmem()),
    )
    turned[1] = exchange(after(x, turned[2]))
    made[2] = make_grad(2, after(turned[2], x))
    sums[2] = reduce_groups(after(made[2], turned[1]))
    made[1] = make_grad(1, after(turned[1], made[2]))
    dz = call(
        functools.partial(backward_conv, reach - ext_da), "backward_conv",
        sds((frames, entry_width), bf16),
        [any_()] * 4,
        [
            wide_rows(rows, channels, bf16), seg_rows, wide_rows(frames, entry_width), planes(rows, channels),
            pltpu.VMEM((taps, channels, entry_width), bf16), wide_rows(frames, entry_width),
            wide_rows(frames, entry_width, bf16), sems(taps + 4),
        ],
        *conv_cost(frames, entry_width), (after(da, made[1]), seg, w_first, res_entry), any_(),
    )
    while len(res_part.order) > 1:
        res_part.step(turned[1])
    others = {n: fetch(after(sums[n], x)) for n in range(layers, 3, -1)}
    others[2] = fetch(sums[2])
    sums[1] = halve_groups(made[1], dz, others[2])
    others[3] = fetch(after(sums[3], made[1]))
    res_part.step(dz)
    res_share = res_part.part[0]
    res_other = fetch(res_share)
    others[1] = fetch(sums[1])
    for layer in range(layers, 0, -1):
        grads[layer] = joined(sums[layer], others[layer])
    grad_res_weight = added(res_share, res_other)

    grad_block_input = dz[None]

    def share(v):
        return lax.dynamic_slice_in_dim(v, place * unit, unit, axis=v.ndim - 1)

    norm_sums = share(jnp.stack(totals[1:]).reshape(layers, 2, channels))
    grad_shift, grad_gain = norm_sums[: layers - 1, 0], norm_sums[:, 1]
    grad_last_shift = norm_sums[layers - 1, 0]
    grad_res_gain = share(res_tot[: 3 * blocks].reshape(3, channels))
    grad_res_shift = jnp.broadcast_to(grad_last_shift[None], (3, unit))
    grad_w_first = jnp.transpose(grads[1], (1, 0, 2))
    grad_w_rest = jnp.transpose(jnp.stack(grads[2:]), (0, 2, 1, 3))
    return (
        block_output[None],
        grad_block_input,
        prelude_gradient[None],
        grad_first[None],
        grad_w_first,
        grad_w_rest,
        grad_gain,
        grad_shift,
        grad_last_shift,
        grad_res_weight,
        grad_res_gain,
        grad_res_shift,
    )


def solution(mesh):
    split = P("batch", "tm", None)
    in_specs = (
        split, split, split, P("batch", None), P(), P(), P(), P(), P(), P(), P(), split,
    )
    out_specs = (
        split, split, split, split,
        P("tm", None, None), P(None, "tm", None, None), P(None, "tm"), P(None, "tm"), P("tm"),
        P("tm", None), P(None, "tm"), P(None, "tm"),
    )
    return jax.shard_map(
        per_device, mesh=mesh, in_specs=in_specs, out_specs=out_specs, check_vma=False
    )
```

profile of v0, /device:TPU:0, one launch (start us, length us, event | category | flops | bytes accessed | tf_op | source)
XLA Modules:
  0.0 388.0 jit_solution(11238356194071653594)
XLA Ops:
  14.5 2.8 branch_sums.1.rest_0_
  19.7 9.7 %forward_first.1 = (f32[656,512]{1,0:T(8,128)}, f32[32,8,128]{2,1,0:T(8,128)}) custom-call(bf16[512,384]{1,0:T(8,128)(2,1)} %bitcast.98, bf16[80,384]{1,0:T(8,128)(2,1)} %copy-done.18, bf16[80,384]{1,0:T(8,128)(2,1)} %copy-done.19, f32[672,128]{1,0:T(8,128)} %get-tuple-element.105.seg_hbm, bf16[17,512,384]{2,1,0:T(8,128)(2,1)} %bitcast.127), custom_call_target="tpu_custom_call" | custom-call | flops 4385144832 | bytes 9371648 | tf_op jit(solution)/shard_map/forward_first/pallas_call | solution.py:600
  29.5 7.5 %all-to-all-start = ((f32[32,8,128]{2,1,0:T(8,128)}), f32[32,8,128]{2,1,0:T(8,128)S(1)}, u32[]{:S(2)}, u32[]{:S(2)}) async-start(f32[32,8,128]{2,1,0:T(8,128)} %get-tuple-element.107), calls=%async_computation | async-start | bytes 262144 | tf_op jit(solution)/shard_map/all_to_all | solution.py:661
  39.5 2.5 chunk_segments.1.segs_ref
  41.9 3.7 all-to-all-done.st_hbm.prev_st_hbm
  46.2 10.1 %forward_next.4 = (f32[640,512]{1,0:T(8,128)}, bf16[512,512]{1,0:T(8,128)(2,1)}, f32[32,16,128]{2,1,0:T(8,128)}) custom-call(f32[656,512]{1,0:T(8,128)} %get-tuple-element.106.prev_hbm.a_hbm, f32[32,8,128]{2,1,0:T(8,128)} %copy-done.1, f32[5,512]{1,0:T(8,128)} %gain_hbm.17, f32[5,512]{1,0:T(8,128)} %shift_hbm.15, f32[672,128]{1,0:T(8,128)} %get-tuple-element.105.seg_hbm, ...), custom_call_target="tpu_custom_call" | custom-call | flops 5704253440 | bytes 11534336 | tf_op jit(solution)/shard_map/forward_next/pallas_call | solution.py:600
  56.3 14.0 %all_to_all.80.st_hbm.q0_hbm.prev_st_hbm = f32[32,16,128]{2,1,0:T(8,128)} all-to-all(f32[32,16,128]{2,1,0:T(8,128)} %get-tuple-element.112), channel_id=1, replica_groups=mesh['tm'=16,'batch'=2] {'tm','batch'}, dimensions={0} | all-to-all | bytes 524288 | tf_op jit(solution)/shard_map/all_to_all | solution.py:661
  70.4 9.9 %forward_next.5 = (f32[624,512]{1,0:T(8,128)}, bf16[512,512]{1,0:T(8,128)(2,1)}, f32[32,16,128]{2,1,0:T(8,128)}) custom-call(f32[640,512]{1,0:T(8,128)} %get-tuple-element.111.prev_hbm.a_hbm, f32[32,16,128]{2,1,0:T(8,128)} %all_to_all.80.st_hbm.q0_hbm.prev_st_hbm, f32[5,512]{1,0:T(8,128)} %gain_hbm.17, f32[5,512]{1,0:T(8,128)} %shift_hbm.15, ...), custom_call_target="tpu_custom_call" | custom-call | flops 5561647104 | bytes 11468800 | tf_op jit(solution)/shard_map/forward_next/pallas_call | solution.py:600
  80.3 14.4 %all_to_all.81.st_hbm.q1_hbm.prev_st_hbm = f32[32,16,128]{2,1,0:T(8,128)} all-to-all(f32[32,16,128]{2,1,0:T(8,128)} %get-tuple-element.114), channel_id=1, replica_groups=mesh['tm'=16,'batch'=2] {'tm','batch'}, dimensions={0} | all-to-all | bytes 524288 | tf_op jit(solution)/shard_map/all_to_all | solution.py:661
  94.7 9.8 %forward_next.6 = (f32[608,512]{1,0:T(8,128)}, bf16[512,512]{1,0:T(8,128)(2,1)}, f32[32,16,128]{2,1,0:T(8,128)}) custom-call(f32[624,512]{1,0:T(8,128)} %get-tuple-element.113.prev_hbm.a_hbm, f32[32,16,128]{2,1,0:T(8,128)} %all_to_all.81.st_hbm.q1_hbm.prev_st_hbm, f32[5,512]{1,0:T(8,128)} %gain_hbm.17, f32[5,512]{1,0:T(8,128)} %shift_hbm.15, ...), custom_call_target="tpu_custom_call" | custom-call | flops 5419040768 | bytes 11403264 | tf_op jit(solution)/shard_map/forward_next/pallas_call | solution.py:600
  104.6 2.6 all-to-all-start.3
  110.6 3.0 collective-permute-done.4.sh_hbm
  113.6 4.2 %all-to-all-done.3.st_hbm.q2_hbm.prev_st_hbm = f32[32,16,128]{2,1,0:T(8,128)S(1)} async-done(((f32[32,16,128]{2,1,0:T(8,128)}), f32[32,16,128]{2,1,0:T(8,128)S(1)}, u32[]{:S(2)}, u32[]{:S(2)}) %all-to-all-start.3) | async-done | bytes 262176 | tf_op jit(solution)/shard_map/all_to_all | solution.py:661
  118.6 9.6 %forward_next.7 = (f32[592,512]{1,0:T(8,128)}, bf16[512,512]{1,0:T(8,128)(2,1)}, f32[32,8,128]{2,1,0:T(8,128)}) custom-call(f32[608,512]{1,0:T(8,128)} %get-tuple-element.115.prev_hbm.a_hbm, f32[32,16,128]{2,1,0:T(8,128)} %copy-done, f32[5,512]{1,0:T(8,128)} %gain_hbm.17, f32[5,512]{1,0:T(8,128)} %shift_hbm.15, f32[672,128]{1,0:T(8,128)} %get-tuple-element.105.seg_hbm, ...), custom_call_target="tpu_custom_call" | custom-call | flops 5276434432 | bytes 11337728 | tf_op jit(solution)/shard_map/forward_next/pallas_call | solution.py:600
  128.2 13.1 %all_to_all.82.st_hbm = f32[32,8,128]{2,1,0:T(8,128)} all-to-all(f32[32,8,128]{2,1,0:T(8,128)} %get-tuple-element.120), channel_id=1, replica_groups=mesh['tm'=16,'batch'=2] {'tm','batch'}, dimensions={0} | all-to-all | bytes 262144 | tf_op jit(solution)/shard_map/all_to_all | solution.py:661
  141.9 7.1 %join.1 = (bf16[512,512]{1,0:T(8,128)(2,1)}, f32[592,512]{1,0:T(8,128)}, f32[32,8,128]{2,1,0:T(8,128)}, f32[32,16,128]{2,1,0:T(8,128)}, f32[3,8,128]{2,1,0:T(8,128)}) custom-call(f32[592,512]{1,0:T(8,128)} %get-tuple-element.119.a_hbm, f32[32,8,128]{2,1,0:T(8,128)} %all_to_all.82.st_hbm, bf16[512,256]{1,0:T(8,128)(2,1)} %bitcast.103, ...), custom_call_target="tpu_custom_call" | custom-call | flops 543162368 | bytes 8388608 | tf_op jit(solution)/shard_map/join/pallas_call | solution.py:600
  149.0 11.9 %all_to_all.83.bst_hbm.bst_ref = f32[32,8,128]{2,1,0:T(8,128)} all-to-all(f32[32,8,128]{2,1,0:T(8,128)} %get-tuple-element.126), channel_id=1, replica_groups=mesh['tm'=16,'batch'=2] {'tm','batch'}, dimensions={0} | all-to-all | bytes 262144 | tf_op jit(solution)/shard_map/all_to_all | solution.py:661
  160.9 2.6 all-to-all-start.7
  163.5 11.0 %backward_step.4 = (f32[576,512]{1,0:T(8,128)}, bf16[8,272,128]{2,1,0:T(8,128)(2,1)}, f32[8,128]{1,0:T(8,128)}, f32[32,8,128]{2,1,0:T(8,128)}) custom-call(f32[592,512]{1,0:T(8,128)} %get-tuple-element.125.dz_hbm.du_ref, f32[32,8,128]{2,1,0:T(8,128)} %all_to_all.83.bst_hbm.bst_ref, f32[592,512]{1,0:T(8,128)} %get-tuple-element.119.a_hbm, ...), custom_call_target="tpu_custom_call" | custom-call | flops 5133828096 | bytes 11272192 | tf_op jit(solution)/shard_map/backward_step/pallas_call | solution.py:600
  174.5 5.8 %all-to-all-start.6 = ((f32[32,8,128]{2,1,0:T(8,128)}), f32[32,8,128]{2,1,0:T(8,128)S(1)}, u32[]{:S(2)}, u32[]{:S(2)}) async-start(f32[32,8,128]{2,1,0:T(8,128)} %get-tuple-element.131), calls=%async_computation.6 | async-start | bytes 262144 | tf_op jit(solution)/shard_map/all_to_all | solution.py:661
  180.4 5.1 %branch_grads.1 = (bf16[512,256]{1,0:T(8,128)(2,1)}, bf16[512,256]{1,0:T(8,128)(2,1)}, f32[512,384]{1,0:T(8,128)}, bf16[512,896]{1,0:T(8,128)(2,1)}, f32[16,128]{1,0:T(8,128)}) custom-call(f32[592,512]{1,0:T(8,128)} %get-tuple-element.125.dz_hbm.du_ref, f32[32,8,128]{2,1,0:T(8,128)} %all_to_all.83.bst_hbm.bst_ref, f32[32,16,128]{2,1,0:T(8,128)} %copy-done.15, ...), custom_call_target="tpu_custom_call" | custom-call | flops 1409286144 | bytes 8388608 | tf_op jit(solution)/shard_map/branch_grads/pallas_call | solution.py:600
  185.5 3.5 all-to-all-done.6.bst_hbm
  189.0 3.8 all-to-all-start.8
  194.4 10.7 %backward_step.5 = (f32[560,512]{1,0:T(8,128)}, bf16[8,272,128]{2,1,0:T(8,128)(2,1)}, f32[8,128]{1,0:T(8,128)}, f32[32,8,128]{2,1,0:T(8,128)}) custom-call(f32[576,512]{1,0:T(8,128)} %get-tuple-element.130.dz_hbm, f32[32,8,128]{2,1,0:T(8,128)} %copy-done.10, f32[608,512]{1,0:T(8,128)} %get-tuple-element.115.prev_hbm.a_hbm, f32[32,16,128]{2,1,0:T(8,128)} %copy-done, ...), custom_call_target="tpu_custom_call" | custom-call | flops 4991221760 | bytes 11206656 | tf_op jit(solution)/shard_map/backward_step/pallas_call | solution.py:600
  205.1 2.8 all-to-all-done.8.x_ref
  207.9 2.6 all-to-all-start.9
  210.6 9.8 %weight_grads.5 = bf16[4,17,16,512]{3,2,1,0:T(8,128)(2,1)} custom-call(bf16[8,272,128]{2,1,0:T(8,128)(2,1)} %copy-done.6, bf16[8,528,128]{2,1,0:T(8,128)(2,1)} %chunk_segments.1.segs_ref, bf16[8,512,512]{2,1,0:T(8,128)(2,1)} %bitcast.132), custom_call_target="tpu_custom_call" | custom-call | flops 4563402752 | bytes 4194304 | tf_op jit(solution)/shard_map/weight_grads/pallas_call | solution.py:600
  220.4 4.3 %all-to-all-start.10 = ((bf16[8,272,128]{2,1,0:T(8,128)(2,1)}), bf16[8,272,128]{2,1,0:T(8,128)(2,1)S(1)}, u32[]{:S(2)}, u32[]{:S(2)}) async-start(bf16[8,272,128]{2,1,0:T(8,128)(2,1)} %get-tuple-element.151), calls=%async_computation.10 | async-start | bytes 1114112 | tf_op jit(solution)/shard_map/all_to_all | solution.py:836
  224.7 10.7 %backward_step.6 = (f32[544,512]{1,0:T(8,128)}, bf16[8,272,128]{2,1,0:T(8,128)(2,1)}, f32[8,128]{1,0:T(8,128)}, f32[32,8,128]{2,1,0:T(8,128)}) custom-call(f32[560,512]{1,0:T(8,128)} %get-tuple-element.136.dz_hbm, f32[32,8,128]{2,1,0:T(8,128)} %copy-done.11, f32[624,512]{1,0:T(8,128)} %get-tuple-element.113.prev_hbm.a_hbm, ...), custom_call_target="tpu_custom_call" | custom-call | flops 4848615424 | bytes 11141120 | tf_op jit(solution)/shard_map/backward_step/pallas_call | solution.py:600
  235.4 6.1 %all-to-all-start.11 = ((f32[32,8,128]{2,1,0:T(8,128)}), f32[32,8,128]{2,1,0:T(8,128)S(1)}, u32[]{:S(2)}, u32[]{:S(2)}) async-start(f32[32,8,128]{2,1,0:T(8,128)} %get-tuple-element.152), calls=%async_computation.11 | async-start | bytes 262144 | tf_op jit(solution)/shard_map/all_to_all | solution.py:661
  241.6 9.9 %weight_grads.6 = bf16[4,17,16,512]{3,2,1,0:T(8,128)(2,1)} custom-call(bf16[8,272,128]{2,1,0:T(8,128)(2,1)} %copy-done.8, bf16[8,528,128]{2,1,0:T(8,128)(2,1)} %chunk_segments.1.segs_ref, bf16[8,512,512]{2,1,0:T(8,128)(2,1)} %bitcast.131), custom_call_target="tpu_custom_call" | custom-call | flops 4563402752 | bytes 4194304 | tf_op jit(solution)/shard_map/weight_grads/pallas_call | solution.py:600
  252.7 3.7 all-to-all-start.12
  257.5 10.4 %backward_step.7 = (f32[528,512]{1,0:T(8,128)}, bf16[8,272,128]{2,1,0:T(8,128)(2,1)}, f32[8,128]{1,0:T(8,128)}, f32[32,8,128]{2,1,0:T(8,128)}) custom-call(f32[544,512]{1,0:T(8,128)} %get-tuple-element.148.dz_hbm, f32[32,8,128]{2,1,0:T(8,128)} %copy-done.9, f32[640,512]{1,0:T(8,128)} %get-tuple-element.111.prev_hbm.a_hbm, ...), custom_call_target="tpu_custom_call" | custom-call | flops 4706009088 | bytes 11075584 | tf_op jit(solution)/shard_map/backward_step/pallas_call | solution.py:600
  267.9 5.2 %all-to-all-start.13 = ((f32[32,8,128]{2,1,0:T(8,128)}), f32[32,8,128]{2,1,0:T(8,128)S(1)}, u32[]{:S(2)}, u32[]{:S(2)}) async-start(f32[32,8,128]{2,1,0:T(8,128)} %get-tuple-element.163), calls=%async_computation.13 | async-start | bytes 262144 | tf_op jit(solution)/shard_map/all_to_all | solution.py:661
  273.2 9.8 %weight_grads.7 = bf16[4,17,16,512]{3,2,1,0:T(8,128)(2,1)} custom-call(bf16[8,272,128]{2,1,0:T(8,128)(2,1)} %copy-done.7, bf16[8,528,128]{2,1,0:T(8,128)(2,1)} %chunk_segments.1.segs_ref, bf16[8,512,512]{2,1,0:T(8,128)(2,1)} %bitcast.130), custom_call_target="tpu_custom_call" | custom-call | flops 4563402752 | bytes 4194304 | tf_op jit(solution)/shard_map/weight_grads/pallas_call | solution.py:600
  285.0 4.0 %backward_norm.1 = (bf16[528,512]{1,0:T(8,128)(2,1)}, bf16[8,272,128]{2,1,0:T(8,128)(2,1)}, f32[8,128]{1,0:T(8,128)}) custom-call(f32[528,512]{1,0:T(8,128)} %get-tuple-element.157.dz_hbm, f32[32,8,128]{2,1,0:T(8,128)} %copy-done.12, f32[656,512]{1,0:T(8,128)} %get-tuple-element.106.prev_hbm.a_hbm, f32[32,8,128]{2,1,0:T(8,128)} %copy-done.1, f32[5,512]{1,0:T(8,128)} %gain_hbm.17), custom_call_target="tpu_custom_call" | custom-call | flops 1000 | bytes 4194304 | tf_op jit(solution)/shard_map/backward_norm/pallas_call | solution.py:600
  289.0 3.5 all-to-all-start.14
  298.5 3.6 all-to-all-done.14.x_ref
  302.1 3.5 all-to-all-start.15
  306.0 9.8 %weight_grads.8 = bf16[4,17,16,512]{3,2,1,0:T(8,128)(2,1)} custom-call(bf16[8,272,128]{2,1,0:T(8,128)(2,1)} %copy-done.4, bf16[8,528,128]{2,1,0:T(8,128)(2,1)} %chunk_segments.1.segs_ref, bf16[8,512,512]{2,1,0:T(8,128)(2,1)} %bitcast.129), custom_call_target="tpu_custom_call" | custom-call | flops 4563402752 | bytes 4194304 | tf_op jit(solution)/shard_map/weight_grads/pallas_call | solution.py:600
  317.9 9.7 %weight_grads.9 = bf16[4,17,16,384]{3,2,1,0:T(8,128)(2,1)} custom-call(bf16[8,272,128]{2,1,0:T(8,128)(2,1)} %copy-done.5, bf16[8,528,128]{2,1,0:T(8,128)(2,1)} %chunk_segments.1.segs_ref, bf16[8,512,384]{2,1,0:T(8,128)(2,1)} %all-gather.10.cloned.1.call-done.h_ref), custom_call_target="tpu_custom_call" | custom-call | flops 3422552064 | bytes 3145728 | tf_op jit(solution)/shard_map/weight_grads/pallas_call | solution.py:600
  331.1 9.9 %backward_conv.1 = bf16[512,384]{1,0:T(8,128)(2,1)} custom-call(bf16[528,512]{1,0:T(8,128)(2,1)} %get-tuple-element.174.da_hbm, f32[672,128]{1,0:T(8,128)} %get-tuple-element.105.seg_hbm, bf16[17,512,384]{2,1,0:T(8,128)(2,1)} %bitcast.128, f32[512,384]{1,0:T(8,128)} %get-tuple-element.175.add_hbm), custom_call_target="tpu_custom_call" | custom-call | flops 3422552064 | bytes 8781824 | tf_op jit(solution)/shard_map/backward_conv/pallas_call | solution.py:600
  341.8 3.5 collective-permute-done.16
  346.0 11.1 %collective-permute-done.7 = bf16[2,17,16,384]{3,2,1,0:T(8,128)(2,1)S(1)} collective-permute-done((bf16[2,17,16,384]{3,2,1,0:T(8,128)(2,1)S(1)}, bf16[2,17,16,384]{3,2,1,0:T(8,128)(2,1)S(1)}, u32[]{:S(2)}, u32[]{:S(2)}) %collective-permute-start.7) | collective-permute-done | bytes 417824 | tf_op jit(solution)/shard_map/ppermute | solution.py:658
  361.7 3.5 collective-permute-done.11
  366.3 5.9 %collective-permute-done.8 = bf16[17,16,384]{2,1,0:T(8,128)(2,1)S(1)} collective-permute-done((bf16[17,16,384]{2,1,0:T(8,128)(2,1)S(1)}, bf16[17,16,384]{2,1,0:T(8,128)(2,1)S(1)}, u32[]{:S(2)}, u32[]{:S(2)}) %collective-permute-start.8) | collective-permute-done | bytes 208928 | tf_op jit(solution)/shard_map/ppermute | solution.py:658
  374.5 2.4 convert_bitcast_fusion
  376.9 2.6 collective-permute-done.10
  (152 shorter events, 46.2 us)
Async XLA Ops:
  7.2 110.7 %all-gather.10.cloned.1.call-start = ((), (), s32[]{:S(2)}) async-start(), calls=%async_computation.20 | async-start | bytes 3538944 | tf_op jit(solution)/shard_map/all_gather | solution.py:741
  10.2 7.1 %collective-permute-start = (bf16[80,384]{1,0:T(8,128)(2,1)}, bf16[80,384]{1,0:T(8,128)(2,1)S(1)}, u32[]{:S(2)}, u32[]{:S(2)}) collective-permute-start(bf16[80,384]{1,0:T(8,128)(2,1)} %get-tuple-element.103), channel_id=1, source_target_pairs={{0,2},{2,4},{4,6},{6,8},{8,10},{10,12},{12,14},{14,16},{16,18},{18... | collective-permute-start | bytes 184328 | tf_op jit(solution)/shard_map/ppermute | solution.py:684
  12.6 5.5 %collective-permute-start.1 = (bf16[80,384]{1,0:T(8,128)(2,1)}, bf16[80,384]{1,0:T(8,128)(2,1)S(1)}, u32[]{:S(2)}, u32[]{:S(2)}) collective-permute-start(bf16[80,384]{1,0:T(8,128)(2,1)} %get-tuple-element.104), channel_id=1, source_target_pairs={{2,0},{4,2},{6,4},{8,6},{10,8},{12,10},{14,12},{16,14},{18,16},{20... | collective-permute-start | bytes 184328 | tf_op jit(solution)/shard_map/ppermute | solution.py:684
  18.1 19.1 %collective-permute-start.2 = (s32[1,16]{1,0:T(1,128)}, s32[1,16]{1,0:T(1,128)S(1)}, u32[]{:S(2)}, u32[]{:S(2)}) collective-permute-start(s32[1,16]{1,0:T(1,128)} %counts_ref.1), channel_id=1, source_target_pairs={{0,1},{1,0},{2,3},{3,2},{4,5},{5,4},{6,7},{7,6},{8,9},{9,8},{10,11... | collective-permute-start | bytes 200 | tf_op jit(solution)/shard_map/ppermute | solution.py:658
  19.7 17.5 %copy-start.25 = (s32[1,16]{1,0:T(1,128)S(1)}, s32[1,16]{1,0:T(1,128)}, u32[]{:S(2)}) copy-start(s32[1,16]{1,0:T(1,128)} %counts_ref.1) | copy-start | bytes 196
  29.5 16.1 %all-to-all-start = ((f32[32,8,128]{2,1,0:T(8,128)}), f32[32,8,128]{2,1,0:T(8,128)S(1)}, u32[]{:S(2)}, u32[]{:S(2)}) async-start(f32[32,8,128]{2,1,0:T(8,128)} %get-tuple-element.107), calls=%async_computation | async-start | bytes 262144 | tf_op jit(solution)/shard_map/all_to_all | solution.py:661
  37.0 104.9 %all-gather.12.cloned.1.call-start = ((), (), s32[]{:S(2)}) async-start(), calls=%async_computation.25 | async-start | bytes 4718592 | tf_op jit(solution)/shard_map/all_gather | solution.py:741
  70.3 93.2 %all-gather.14.cloned.1.call-start = ((), (), s32[]{:S(2)}) async-start(), calls=%async_computation.26 | async-start | bytes 4718592 | tf_op jit(solution)/shard_map/all_gather | solution.py:741
  94.7 14.5 %copy-start.27 = (bf16[48,1024]{1,0:T(8,128)(2,1)S(1)}, bf16[48,1024]{1,0:T(8,128)(2,1)}, u32[]{:S(2)}) copy-start(bf16[48,1024]{1,0:T(8,128)(2,1)} %get-tuple-element.117) | copy-start | bytes 294916
  104.6 13.3 %all-to-all-start.3 = ((f32[32,16,128]{2,1,0:T(8,128)}), f32[32,16,128]{2,1,0:T(8,128)S(1)}, u32[]{:S(2)}, u32[]{:S(2)}) async-start(f32[32,16,128]{2,1,0:T(8,128)} %get-tuple-element.116), calls=%async_computation.3 | async-start | bytes 524288 | tf_op jit(solution)/shard_map/all_to_all | solution.py:661
  107.2 103.4 %all-gather.16.cloned.1.call-start = ((), (), s32[]{:S(2)}) async-start(), calls=%async_computation.27 | async-start | bytes 4718592 | tf_op jit(solution)/shard_map/all_gather | solution.py:741
  107.2 3.3 collective-permute-start.3
  109.3 4.4 %collective-permute-start.4 = (bf16[48,1024]{1,0:T(8,128)(2,1)S(1)}, bf16[48,1024]{1,0:T(8,128)(2,1)S(1)}, u32[]{:S(2)}, u32[]{:S(2)}) collective-permute-start(bf16[48,1024]{1,0:T(8,128)(2,1)S(1)} %copy-done.27), channel_id=1, source_target_pairs={{2,0},{4,2},{6,4},{8,6},{10,8},{12,10},{14,12},{16,14},{18,16},{20... | collective-permute-start | bytes 294920 | tf_op jit(solution)/shard_map/ppermute | solution.py:754
  110.6 17.6 %copy-start.16 = (bf16[48,1024]{1,0:T(8,128)(2,1)}, bf16[48,1024]{1,0:T(8,128)(2,1)S(1)}, u32[]{:S(2)}) copy-start(bf16[48,1024]{1,0:T(8,128)(2,1)S(1)} %collective-permute-done.3.sl_hbm) | copy-start | bytes 294916
  113.6 14.5 %copy-start.17 = (bf16[48,1024]{1,0:T(8,128)(2,1)}, bf16[48,1024]{1,0:T(8,128)(2,1)S(1)}, u32[]{:S(2)}) copy-start(bf16[48,1024]{1,0:T(8,128)(2,1)S(1)} %collective-permute-done.4.sh_hbm) | copy-start | bytes 294916
  141.3 100.3 %all-gather.18.cloned.1.call-start = ((), (), s32[]{:S(2)}) async-start(), calls=%async_computation.28 | async-start | bytes 4718592 | tf_op jit(solution)/shard_map/all_gather | solution.py:741
  160.9 13.6 %all-to-all-start.7 = ((f32[32,16,128]{2,1,0:T(8,128)}), f32[32,16,128]{2,1,0:T(8,128)S(1)}, u32[]{:S(2)}, u32[]{:S(2)}) async-start(f32[32,16,128]{2,1,0:T(8,128)} %get-tuple-element.132), calls=%async_computation.7 | async-start | bytes 524288 | tf_op jit(solution)/shard_map/all_to_all | solution.py:661
  174.5 14.5 %all-to-all-start.6 = ((f32[32,8,128]{2,1,0:T(8,128)}), f32[32,8,128]{2,1,0:T(8,128)S(1)}, u32[]{:S(2)}, u32[]{:S(2)}) async-start(f32[32,8,128]{2,1,0:T(8,128)} %get-tuple-element.131), calls=%async_computation.6 | async-start | bytes 262144 | tf_op jit(solution)/shard_map/all_to_all | solution.py:661
  189.0 18.9 %all-to-all-start.8 = ((bf16[8,272,128]{2,1,0:T(8,128)(2,1)}), bf16[8,272,128]{2,1,0:T(8,128)(2,1)S(1)}, u32[]{:S(2)}, u32[]{:S(2)}) async-start(bf16[8,272,128]{2,1,0:T(8,128)(2,1)} %get-tuple-element.139), calls=%async_computation.8 | async-start | bytes 1114112 | tf_op jit(solution)/shard_map/all_to_all | solution.py:836
  193.9 14.1 %collective-permute-start.5 = (bf16[8,1,32,896]{3,2,0,1:T(8,128)(2,1)S(1)}, bf16[8,1,32,896]{3,2,0,1:T(8,128)(2,1)S(1)}, u32[]{:S(2)}, u32[]{:S(2)}) collective-permute-start(bf16[8,1,32,896]{3,2,0,1:T(8,128)(2,1)S(1)} %dynamic-slice_bitcast_fusion), channel_id=1, source_target_pairs={{0,2},{2,0},{4,6},{6,4},{8,10},{10,8},{12,14},{14,12},{16,18},{18,... | collective-permute-start | bytes 1376264 | tf_op jit(solution)/shard_map/ppermute | solution.py:658
  207.9 12.5 %all-to-all-start.9 = ((f32[32,8,128]{2,1,0:T(8,128)}), f32[32,8,128]{2,1,0:T(8,128)S(1)}, u32[]{:S(2)}, u32[]{:S(2)}) async-start(f32[32,8,128]{2,1,0:T(8,128)} %get-tuple-element.143), calls=%async_computation.9 | async-start | bytes 262144 | tf_op jit(solution)/shard_map/all_to_all | solution.py:661
  210.5 74.5 %reduce-scatter.5.cloned.1.call-start = ((), (), s32[]{:S(2)}) async-start(), calls=%async_computation.21 | async-start | bytes 1392640 | tf_op jit(solution)/shard_map/reduce_scatter | solution.py:868
  220.4 15.0 %all-to-all-start.10 = ((bf16[8,272,128]{2,1,0:T(8,128)(2,1)}), bf16[8,272,128]{2,1,0:T(8,128)(2,1)S(1)}, u32[]{:S(2)}, u32[]{:S(2)}) async-start(bf16[8,272,128]{2,1,0:T(8,128)(2,1)} %get-tuple-element.151), calls=%async_computation.10 | async-start | bytes 1114112 | tf_op jit(solution)/shard_map/all_to_all | solution.py:836
  235.4 17.2 %all-to-all-start.11 = ((f32[32,8,128]{2,1,0:T(8,128)}), f32[32,8,128]{2,1,0:T(8,128)S(1)}, u32[]{:S(2)}, u32[]{:S(2)}) async-start(f32[32,8,128]{2,1,0:T(8,128)} %get-tuple-element.152), calls=%async_computation.11 | async-start | bytes 262144 | tf_op jit(solution)/shard_map/all_to_all | solution.py:661
  241.6 74.4 %reduce-scatter.11.cloned.1.call-start = ((), (), s32[]{:S(2)}) async-start(), calls=%async_computation.24 | async-start | bytes 1392640 | tf_op jit(solution)/shard_map/reduce_scatter | solution.py:868
  241.6 14.8 %copy-start.2 = (bf16[512,896]{1,0:T(8,128)(2,1)S(1)}, bf16[512,896]{1,0:T(8,128)(2,1)}, u32[]{:S(2)}) copy-start(bf16[512,896]{1,0:T(8,128)(2,1)} %get-tuple-element.142) | copy-start | bytes 2752516
  252.7 15.2 %all-to-all-start.12 = ((bf16[8,272,128]{2,1,0:T(8,128)(2,1)}), bf16[8,272,128]{2,1,0:T(8,128)(2,1)S(1)}, u32[]{:S(2)}, u32[]{:S(2)}) async-start(bf16[8,272,128]{2,1,0:T(8,128)(2,1)} %get-tuple-element.160), calls=%async_computation.12 | async-start | bytes 1114112 | tf_op jit(solution)/shard_map/all_to_all | solution.py:836
  256.6 11.3 %collective-permute-start.6 = (bf16[2,2,32,896]{3,2,1,0:T(8,128)(2,1)S(1)}, bf16[2,2,32,896]{3,2,1,0:T(8,128)(2,1)S(1)}, u32[]{:S(2)}, u32[]{:S(2)}) collective-permute-start(bf16[2,2,32,896]{3,2,1,0:T(8,128)(2,1)S(1)} %dynamic-slice_bitcast_fusion.2), channel_id=1, source_target_pairs={{0,8},{2,10},{4,12},{6,14},{8,0},{10,2},{12,4},{14,6},{16,24},{18,... | collective-permute-start | bytes 688136 | tf_op jit(solution)/shard_map/ppermute | solution.py:658
  267.9 16.2 %all-to-all-start.13 = ((f32[32,8,128]{2,1,0:T(8,128)}), f32[32,8,128]{2,1,0:T(8,128)S(1)}, u32[]{:S(2)}, u32[]{:S(2)}) async-start(f32[32,8,128]{2,1,0:T(8,128)} %get-tuple-element.163), calls=%async_computation.13 | async-start | bytes 262144 | tf_op jit(solution)/shard_map/all_to_all | solution.py:661
  273.1 83.9 %reduce-scatter.9.cloned.1.call-start = ((), (), s32[]{:S(2)}) async-start(), calls=%async_computation.23 | async-start | bytes 1392640 | tf_op jit(solution)/shard_map/reduce_scatter | solution.py:868
  283.0 13.5 %copy-start.21 = (f32[8,128]{1,0:T(8,128)S(1)}, f32[8,128]{1,0:T(8,128)}, u32[]{:S(2)}) copy-start(f32[8,128]{1,0:T(8,128)} %get-tuple-element.189) | copy-start | bytes 12292
  283.0 13.5 %copy-start.22 = (f32[8,128]{1,0:T(8,128)S(1)}, f32[8,128]{1,0:T(8,128)}, u32[]{:S(2)}) copy-start(f32[8,128]{1,0:T(8,128)} %get-tuple-element.188) | copy-start | bytes 12292
  283.0 13.4 %copy-start.23 = (f32[8,128]{1,0:T(8,128)S(1)}, f32[8,128]{1,0:T(8,128)}, u32[]{:S(2)}) copy-start(f32[8,128]{1,0:T(8,128)} %get-tuple-element.187) | copy-start | bytes 12292
  289.0 13.1 %all-to-all-start.14 = ((bf16[8,272,128]{2,1,0:T(8,128)(2,1)}), bf16[8,272,128]{2,1,0:T(8,128)(2,1)S(1)}, u32[]{:S(2)}, u32[]{:S(2)}) async-start(bf16[8,272,128]{2,1,0:T(8,128)(2,1)} %get-tuple-element.170), calls=%async_computation.15 | async-start | bytes 1114112 | tf_op jit(solution)/shard_map/all_to_all | solution.py:836
  292.6 23.3 %collective-permute-start.13 = (bf16[17,16,512]{2,1,0:T(8,128)(2,1)S(1)}, bf16[17,16,512]{2,1,0:T(8,128)(2,1)S(1)}, u32[]{:S(2)}, u32[]{:S(2)}) collective-permute-start(bf16[17,16,512]{2,1,0:T(8,128)(2,1)S(1)} %bitcast.118), channel_id=1, source_target_pairs={{0,1},{1,0},{2,3},{3,2},{4,5},{5,4},{6,7},{7,6},{8,9},{9,8},{10,11... | collective-permute-start | bytes 835592 | tf_op jit(solution)/shard_map/ppermute | solution.py:658
  294.6 34.9 %collective-permute-start.14 = (bf16[1,2,32,896]{3,2,1,0:T(8,128)(2,1)S(1)}, bf16[1,2,32,896]{3,2,1,0:T(8,128)(2,1)S(1)}, u32[]{:S(2)}, u32[]{:S(2)}) collective-permute-start(bf16[1,2,32,896]{3,2,1,0:T(8,128)(2,1)S(1)} %constant_dynamic-slice_fusion.3), channel_id=1, source_target_pairs={{0,16},{2,18},{4,20},{6,22},{8,24},{10,26},{12,28},{14,30},{16,0},... | collective-permute-start | bytes 344072 | tf_op jit(solution)/shard_map/ppermute | solution.py:658
  302.1 13.7 %all-to-all-start.15 = ((bf16[8,272,128]{2,1,0:T(8,128)(2,1)}), bf16[8,272,128]{2,1,0:T(8,128)(2,1)S(1)}, u32[]{:S(2)}, u32[]{:S(2)}) async-start(bf16[8,272,128]{2,1,0:T(8,128)(2,1)} %get-tuple-element.171), calls=%async_computation.16 | async-start | bytes 1114112 | tf_op jit(solution)/shard_map/all_to_all | solution.py:836
  305.7 53.7 %reduce-scatter.7.cloned.1.call-start = ((), (), s32[]{:S(2)}) async-start(), calls=%async_computation.22 | async-start | bytes 1392640 | tf_op jit(solution)/shard_map/reduce_scatter | solution.py:868
  306.0 74.4 %copy-start.26 = (f32[32]{0:T(128)}, f32[32]{0:T(128)S(1)}, u32[]{:S(2)}) copy-start(f32[32]{0:T(128)S(1)} %fusion.6) | copy-start | bytes 388
  315.9 25.8 %collective-permute-start.12 = (bf16[17,16,512]{2,1,0:T(8,128)(2,1)}, bf16[17,16,512]{2,1,0:T(8,128)(2,1)S(1)}, u32[]{:S(2)}, u32[]{:S(2)}) collective-permute-start(bf16[17,16,512]{2,1,0:T(8,128)(2,1)} %bitcast.117), channel_id=1, source_target_pairs={{0,1},{1,0},{2,3},{3,2},{4,5},{5,4},{6,7},{7,6},{8,9},{9,8},{10,11... | collective-permute-start | bytes 835592 | tf_op jit(solution)/shard_map/ppermute | solution.py:658
  328.6 28.4 %collective-permute-start.7 = (bf16[2,17,16,384]{3,2,1,0:T(8,128)(2,1)S(1)}, bf16[2,17,16,384]{3,2,1,0:T(8,128)(2,1)S(1)}, u32[]{:S(2)}, u32[]{:S(2)}) collective-permute-start(bf16[2,17,16,384]{3,2,1,0:T(8,128)(2,1)S(1)} %dynamic-slice_bitcast_fusion.1), channel_id=1, source_target_pairs={{0,8},{2,10},{4,12},{6,14},{8,0},{10,2},{12,4},{14,6},{16,24},{18,... | collective-permute-start | bytes 1253384 | tf_op jit(solution)/shard_map/ppermute | solution.py:658
  329.6 11.5 %collective-permute-start.15 = (bf16[1,1,32,896]{3,2,1,0:T(8,128)(2,1)S(1)}, bf16[1,1,32,896]{3,2,1,0:T(8,128)(2,1)S(1)}, u32[]{:S(2)}, u32[]{:S(2)}) collective-permute-start(bf16[1,1,32,896]{3,2,1,0:T(8,128)(2,1)S(1)} %constant_dynamic-slice_fusion.2), channel_id=1, source_target_pairs={{0,4},{2,6},{4,0},{6,2},{8,12},{10,14},{12,8},{14,10},{16,20},{18,... | collective-permute-start | bytes 172040 | tf_op jit(solution)/shard_map/ppermute | solution.py:658
  331.1 25.9 %copy-start.3 = (bf16[4,17,16,384]{3,2,1,0:T(8,128)(2,1)S(1)}, bf16[4,17,16,384]{3,2,1,0:T(8,128)(2,1)}, u32[]{:S(2)}) copy-start(bf16[4,17,16,384]{3,2,1,0:T(8,128)(2,1)} %weight_grads.9) | copy-start | bytes 2506756
  341.1 4.2 %collective-permute-start.16 = (bf16[32,896]{1,0:T(8,128)(2,1)S(1)}, bf16[32,896]{1,0:T(8,128)(2,1)S(1)}, u32[]{:S(2)}, u32[]{:S(2)}) collective-permute-start(bf16[32,896]{1,0:T(8,128)(2,1)S(1)} %fusion.4), channel_id=1, source_target_pairs={{0,1},{1,0},{2,3},{3,2},{4,5},{5,4},{6,7},{7,6},{8,9},{9,8},{10,11... | collective-permute-start | bytes 172040 | tf_op jit(solution)/shard_map/ppermute | solution.py:658
  357.1 8.2 %collective-permute-start.11 = (bf16[17,16,512]{2,1,0:T(8,128)(2,1)}, bf16[17,16,512]{2,1,0:T(8,128)(2,1)S(1)}, u32[]{:S(2)}, u32[]{:S(2)}) collective-permute-start(bf16[17,16,512]{2,1,0:T(8,128)(2,1)} %bitcast.119), channel_id=1, source_target_pairs={{0,1},{1,0},{2,3},{3,2},{4,5},{5,4},{6,7},{7,6},{8,9},{9,8},{10,11... | collective-permute-start | bytes 835592 | tf_op jit(solution)/shard_map/ppermute | solution.py:658
  359.4 12.8 %collective-permute-start.9 = (bf16[17,16,512]{2,1,0:T(8,128)(2,1)}, bf16[17,16,512]{2,1,0:T(8,128)(2,1)S(1)}, u32[]{:S(2)}, u32[]{:S(2)}) collective-permute-start(bf16[17,16,512]{2,1,0:T(8,128)(2,1)} %bitcast.120), channel_id=1, source_target_pairs={{0,1},{1,0},{2,3},{3,2},{4,5},{5,4},{6,7},{7,6},{8,9},{9,8},{10,11... | collective-permute-start | bytes 835592 | tf_op jit(solution)/shard_map/ppermute | solution.py:658
  360.3 11.9 %collective-permute-start.8 = (bf16[17,16,384]{2,1,0:T(8,128)(2,1)S(1)}, bf16[17,16,384]{2,1,0:T(8,128)(2,1)S(1)}, u32[]{:S(2)}, u32[]{:S(2)}) collective-permute-start(bf16[17,16,384]{2,1,0:T(8,128)(2,1)S(1)} %dynamic-slice_bitcast_fusion.3), channel_id=1, source_target_pairs={{0,16},{2,18},{4,20},{6,22},{8,24},{10,26},{12,28},{14,30},{16,0},... | collective-permute-start | bytes 626696 | tf_op jit(solution)/shard_map/ppermute | solution.py:658
  372.3 7.2 %collective-permute-start.10 = (bf16[17,16,384]{2,1,0:T(8,128)(2,1)S(1)}, bf16[17,16,384]{2,1,0:T(8,128)(2,1)S(1)}, u32[]{:S(2)}, u32[]{:S(2)}) collective-permute-start(bf16[17,16,384]{2,1,0:T(8,128)(2,1)S(1)} %fusion.3), channel_id=1, source_target_pairs={{0,1},{1,0},{2,3},{3,2},{4,5},{5,4},{6,7},{7,6},{8,9},{9,8},{10,11... | collective-permute-start | bytes 626696 | tf_op jit(solution)/shard_map/ppermute | solution.py:658
  (19 other events, 102.2 us)
Sparse Core Ops, SparseCore 0:
  9.9 36.3 all-gather.9
  70.4 34.6 all-gather.11
  107.6 37.9 all-gather.13
  147.4 37.0 all-gather.15
  186.2 40.4 all-gather.17
  228.9 30.3 reduce-scatter.4
  261.7 28.9 reduce-scatter.10
  293.0 27.6 reduce-scatter.8
  323.7 35.6 reduce-scatter.6
where the time goes:
time: 394 us; the launch traced here: 388 us
  Pallas kernels  176 us (45%)
  starting transfers between devices  74.5 us (19%)
  waiting for transfers between devices  54 us (14%)
  blocking collectives  53.4 us (14%)
  between operations  15.3 us (4%)
  other arithmetic  7.72 us (2%)
  local copies, waits for them, and re-layouts  7.07 us (2%)
    pallas_call x22, Pallas kernels, call(): pl.pallas_call(body, out_shape=out_shape, in_specs=in_specs, out_specs=ou...  176 us
    all_to_all x4, blocking collectives, spread(): return lax.all_to_all(v, everyone, 0, 0, tiled=True)  53.4 us
    all_to_all x7, starting transfers between devices, spread(): return lax.all_to_all(v, everyone, 0, 0, tiled=True)  32.4 us
    ppermute x13, waiting for transfers between devices, swap(): return lax.ppermute(v, axis, [(i, i ^ bit) for i in range(n)])  26.6 us
    all_to_all x5, starting transfers between devices, exchange(): lax.all_to_all(x, everyone, 0, 0, tiled=True, axis_index_groups=groups)  18.8 us
    ppermute x13, starting transfers between devices, swap(): return lax.ppermute(v, axis, [(i, i ^ bit) for i in range(n)])  15.3 us
    all_to_all x7, waiting for transfers between devices, spread(): return lax.all_to_all(v, everyone, 0, 0, tiled=True)  13.7 us
  transfers between devices with their start and end apart: 38, of which 15 were waited for; matrix products, arithmetic and copies ran while one was open for 3% of the time, Pallas kernels for 45%

commit v1 on v0

--- a/solution.py
+++ b/solution.py
@@ -979,7 +979,7 @@
     ext_da = half_taps
     rows = frames + 2 * ext_da
     made[3] = make_grad(3, after(turned[3], sent[1]))
-    sums[3] = reduce_groups(after(made[3], back[1]))
+    sums[3] = reduce_groups(made[3])
     bst = after(back[1], made[3], sums[layers])
     res_part.step(bst)
     turned[2] = exchange(after(xs[2], bst))

time: 394 us -> 395 us (level)
    ppermute x13, waiting for transfers between devices: 26.6 us -> 18.4 us  [swap(): return lax.ppermute(v, axis, [(i, i ^ bit) for i in range(n)])]
    all_to_all x7, waiting for transfers between devices: 13.7 us -> 20.4 us  [spread(): return lax.all_to_all(v, everyone, 0, 0, tiled=True)]
  transfers between devices with their start and end apart: 38 -> 38, of which waited for: 15 -> 14; matrix products, arithmetic and copies ran while one was open for 3% -> 3% of each run, Pallas kernels for 45% -> 45%
where the time goes in v1:
time: 395 us; the launch traced here: 388 us
  Pallas kernels  176 us (45%)
  starting transfers between devices  72.2 us (18%)
  waiting for transfers between devices  55.3 us (14%)
  blocking collectives  53.4 us (14%)
  between operations  15.3 us (4%)
  local copies, waits for them, and re-layouts  8.49 us (2%)
  other arithmetic  7.72 us (2%)
    pallas_call x22, Pallas kernels, call(): pl.pallas_call(body, out_shape=out_shape, in_specs=in_specs, out_specs=ou...  176 us
    all_to_all x4, blocking collectives, spread(): return lax.all_to_all(v, everyone, 0, 0, tiled=True)  53.4 us
    all_to_all x7, starting transfers between devices, spread(): return lax.all_to_all(v, everyone, 0, 0, tiled=True)  32.3 us
    all_to_all x7, waiting for transfers between devices, spread(): return lax.all_to_all(v, everyone, 0, 0, tiled=True)  20.4 us
    all_to_all x5, starting transfers between devices, exchange(): lax.all_to_all(x, everyone, 0, 0, tiled=True, axis_index_groups=groups)  18.7 us
    ppermute x13, waiting for transfers between devices, swap(): return lax.ppermute(v, axis, [(i, i ^ bit) for i in range(n)])  18.4 us
    ppermute x13, starting transfers between devices, swap(): return lax.ppermute(v, axis, [(i, i ^ bit) for i in range(n)])  13.1 us
    all_to_all x5, waiting for transfers between devices, exchange(): lax.all_to_all(x, everyone, 0, 0, tiled=True, axis_index_groups=groups)  7.9 us
  transfers between devices with their start and end apart: 38, of which 14 were waited for; matrix products, arithmetic and copies ran while one was open for 3% of the time, Pallas kernels for 45%

profile of v1, /device:TPU:0, one launch (start us, length us, event | category | flops | bytes accessed | tf_op | source)
XLA Modules:
  0.0 388.4 jit_solution(6619201182599234756)
XLA Ops:
  14.5 2.8 branch_sums.1.rest_0_
  19.7 9.7 %forward_first.1 = (f32[656,512]{1,0:T(8,128)}, f32[32,8,128]{2,1,0:T(8,128)}) custom-call(bf16[512,384]{1,0:T(8,128)(2,1)} %bitcast.98, bf16[80,384]{1,0:T(8,128)(2,1)} %copy-done.18, bf16[80,384]{1,0:T(8,128)(2,1)} %copy-done.19, f32[672,128]{1,0:T(8,128)} %get-tuple-element.104.seg_hbm, bf16[17,512,384]{2,1,0:T(8,128)(2,1)} %bitcast.127), custom_call_target="tpu_custom_call" | custom-call | flops 4385144832 | bytes 9371648 | tf_op jit(solution)/shard_map/forward_first/pallas_call | solution.py:600
  29.5 7.5 %all-to-all-start = ((f32[32,8,128]{2,1,0:T(8,128)}), f32[32,8,128]{2,1,0:T(8,128)S(1)}, u32[]{:S(2)}, u32[]{:S(2)}) async-start(f32[32,8,128]{2,1,0:T(8,128)} %get-tuple-element.106), calls=%async_computation | async-start | bytes 262144 | tf_op jit(solution)/shard_map/all_to_all | solution.py:661
  39.5 2.5 chunk_segments.1.segs_ref
  41.9 3.7 all-to-all-done.st_hbm.prev_st_hbm
  46.2 10.1 %forward_next.4 = (f32[640,512]{1,0:T(8,128)}, bf16[512,512]{1,0:T(8,128)(2,1)}, f32[32,16,128]{2,1,0:T(8,128)}) custom-call(f32[656,512]{1,0:T(8,128)} %get-tuple-element.105.prev_hbm.a_hbm, f32[32,8,128]{2,1,0:T(8,128)} %copy-done.1, f32[5,512]{1,0:T(8,128)} %gain_hbm.17, f32[5,512]{1,0:T(8,128)} %shift_hbm.15, f32[672,128]{1,0:T(8,128)} %get-tuple-element.104.seg_hbm, ...), custom_call_target="tpu_custom_call" | custom-call | flops 5704253440 | bytes 11534336 | tf_op jit(solution)/shard_map/forward_next/pallas_call | solution.py:600
  56.3 14.0 %all_to_all.80.st_hbm.q0_hbm.prev_st_hbm = f32[32,16,128]{2,1,0:T(8,128)} all-to-all(f32[32,16,128]{2,1,0:T(8,128)} %get-tuple-element.111), channel_id=1, replica_groups=mesh['tm'=16,'batch'=2] {'tm','batch'}, dimensions={0} | all-to-all | bytes 524288 | tf_op jit(solution)/shard_map/all_to_all | solution.py:661
  70.4 9.9 %forward_next.5 = (f32[624,512]{1,0:T(8,128)}, bf16[512,512]{1,0:T(8,128)(2,1)}, f32[32,16,128]{2,1,0:T(8,128)}) custom-call(f32[640,512]{1,0:T(8,128)} %get-tuple-element.110.prev_hbm.a_hbm, f32[32,16,128]{2,1,0:T(8,128)} %all_to_all.80.st_hbm.q0_hbm.prev_st_hbm, f32[5,512]{1,0:T(8,128)} %gain_hbm.17, f32[5,512]{1,0:T(8,128)} %shift_hbm.15, ...), custom_call_target="tpu_custom_call" | custom-call | flops 5561647104 | bytes 11468800 | tf_op jit(solution)/shard_map/forward_next/pallas_call | solution.py:600
  80.3 14.4 %all_to_all.81.st_hbm.q1_hbm.prev_st_hbm = f32[32,16,128]{2,1,0:T(8,128)} all-to-all(f32[32,16,128]{2,1,0:T(8,128)} %get-tuple-element.113), channel_id=1, replica_groups=mesh['tm'=16,'batch'=2] {'tm','batch'}, dimensions={0} | all-to-all | bytes 524288 | tf_op jit(solution)/shard_map/all_to_all | solution.py:661
  94.7 9.8 %forward_next.6 = (f32[608,512]{1,0:T(8,128)}, bf16[512,512]{1,0:T(8,128)(2,1)}, f32[32,16,128]{2,1,0:T(8,128)}) custom-call(f32[624,512]{1,0:T(8,128)} %get-tuple-element.112.prev_hbm.a_hbm, f32[32,16,128]{2,1,0:T(8,128)} %all_to_all.81.st_hbm.q1_hbm.prev_st_hbm, f32[5,512]{1,0:T(8,128)} %gain_hbm.17, f32[5,512]{1,0:T(8,128)} %shift_hbm.15, ...), custom_call_target="tpu_custom_call" | custom-call | flops 5419040768 | bytes 11403264 | tf_op jit(solution)/shard_map/forward_next/pallas_call | solution.py:600
  104.6 2.6 all-to-all-start.3
  110.6 3.0 collective-permute-done.4.sh_hbm
  113.6 4.2 %all-to-all-done.3.st_hbm.q2_hbm.prev_st_hbm = f32[32,16,128]{2,1,0:T(8,128)S(1)} async-done(((f32[32,16,128]{2,1,0:T(8,128)}), f32[32,16,128]{2,1,0:T(8,128)S(1)}, u32[]{:S(2)}, u32[]{:S(2)}) %all-to-all-start.3) | async-done | bytes 262176 | tf_op jit(solution)/shard_map/all_to_all | solution.py:661
  118.6 9.6 %forward_next.7 = (f32[592,512]{1,0:T(8,128)}, bf16[512,512]{1,0:T(8,128)(2,1)}, f32[32,8,128]{2,1,0:T(8,128)}) custom-call(f32[608,512]{1,0:T(8,128)} %get-tuple-element.114.prev_hbm.a_hbm, f32[32,16,128]{2,1,0:T(8,128)} %copy-done, f32[5,512]{1,0:T(8,128)} %gain_hbm.17, f32[5,512]{1,0:T(8,128)} %shift_hbm.15, f32[672,128]{1,0:T(8,128)} %get-tuple-element.104.seg_hbm, ...), custom_call_target="tpu_custom_call" | custom-call | flops 5276434432 | bytes 11337728 | tf_op jit(solution)/shard_map/forward_next/pallas_call | solution.py:600
  128.2 13.1 %all_to_all.82.st_hbm = f32[32,8,128]{2,1,0:T(8,128)} all-to-all(f32[32,8,128]{2,1,0:T(8,128)} %get-tuple-element.119), channel_id=1, replica_groups=mesh['tm'=16,'batch'=2] {'tm','batch'}, dimensions={0} | all-to-all | bytes 262144 | tf_op jit(solution)/shard_map/all_to_all | solution.py:661
  141.9 7.1 %join.1 = (bf16[512,512]{1,0:T(8,128)(2,1)}, f32[592,512]{1,0:T(8,128)}, f32[32,8,128]{2,1,0:T(8,128)}, f32[32,16,128]{2,1,0:T(8,128)}, f32[3,8,128]{2,1,0:T(8,128)}) custom-call(f32[592,512]{1,0:T(8,128)} %get-tuple-element.118.a_hbm, f32[32,8,128]{2,1,0:T(8,128)} %all_to_all.82.st_hbm, bf16[512,256]{1,0:T(8,128)(2,1)} %bitcast.103, ...), custom_call_target="tpu_custom_call" | custom-call | flops 543162368 | bytes 8388608 | tf_op jit(solution)/shard_map/join/pallas_call | solution.py:600
  149.0 11.9 %all_to_all.83.bst_hbm.bst_ref = f32[32,8,128]{2,1,0:T(8,128)} all-to-all(f32[32,8,128]{2,1,0:T(8,128)} %get-tuple-element.125), channel_id=1, replica_groups=mesh['tm'=16,'batch'=2] {'tm','batch'}, dimensions={0} | all-to-all | bytes 262144 | tf_op jit(solution)/shard_map/all_to_all | solution.py:661
  160.9 2.6 all-to-all-start.7
  163.5 11.0 %backward_step.4 = (f32[576,512]{1,0:T(8,128)}, bf16[8,272,128]{2,1,0:T(8,128)(2,1)}, f32[8,128]{1,0:T(8,128)}, f32[32,8,128]{2,1,0:T(8,128)}) custom-call(f32[592,512]{1,0:T(8,128)} %get-tuple-element.124.dz_hbm.du_ref, f32[32,8,128]{2,1,0:T(8,128)} %all_to_all.83.bst_hbm.bst_ref, f32[592,512]{1,0:T(8,128)} %get-tuple-element.118.a_hbm, ...), custom_call_target="tpu_custom_call" | custom-call | flops 5133828096 | bytes 11272192 | tf_op jit(solution)/shard_map/backward_step/pallas_call | solution.py:600
  174.5 5.8 %all-to-all-start.6 = ((f32[32,8,128]{2,1,0:T(8,128)}), f32[32,8,128]{2,1,0:T(8,128)S(1)}, u32[]{:S(2)}, u32[]{:S(2)}) async-start(f32[32,8,128]{2,1,0:T(8,128)} %get-tuple-element.130), calls=%async_computation.6 | async-start | bytes 262144 | tf_op jit(solution)/shard_map/all_to_all | solution.py:661
  180.4 5.1 %branch_grads.1 = (bf16[512,256]{1,0:T(8,128)(2,1)}, bf16[512,256]{1,0:T(8,128)(2,1)}, f32[512,384]{1,0:T(8,128)}, bf16[512,896]{1,0:T(8,128)(2,1)}, f32[16,128]{1,0:T(8,128)}) custom-call(f32[592,512]{1,0:T(8,128)} %get-tuple-element.124.dz_hbm.du_ref, f32[32,8,128]{2,1,0:T(8,128)} %all_to_all.83.bst_hbm.bst_ref, f32[32,16,128]{2,1,0:T(8,128)} %copy-done.15, ...), custom_call_target="tpu_custom_call" | custom-call | flops 1409286144 | bytes 8388608 | tf_op jit(solution)/shard_map/branch_grads/pallas_call | solution.py:600
  185.5 3.5 all-to-all-done.6.bst_hbm
  189.0 3.8 all-to-all-start.8
  194.4 10.7 %backward_step.5 = (f32[560,512]{1,0:T(8,128)}, bf16[8,272,128]{2,1,0:T(8,128)(2,1)}, f32[8,128]{1,0:T(8,128)}, f32[32,8,128]{2,1,0:T(8,128)}) custom-call(f32[576,512]{1,0:T(8,128)} %get-tuple-element.129.dz_hbm, f32[32,8,128]{2,1,0:T(8,128)} %copy-done.10, f32[608,512]{1,0:T(8,128)} %get-tuple-element.114.prev_hbm.a_hbm, f32[32,16,128]{2,1,0:T(8,128)} %copy-done, ...), custom_call_target="tpu_custom_call" | custom-call | flops 4991221760 | bytes 11206656 | tf_op jit(solution)/shard_map/backward_step/pallas_call | solution.py:600
  205.1 2.8 all-to-all-done.8.x_ref
  207.9 2.6 all-to-all-start.9
  210.6 9.8 %weight_grads.5 = bf16[4,17,16,512]{3,2,1,0:T(8,128)(2,1)} custom-call(bf16[8,272,128]{2,1,0:T(8,128)(2,1)} %copy-done.6, bf16[8,528,128]{2,1,0:T(8,128)(2,1)} %chunk_segments.1.segs_ref, bf16[8,512,512]{2,1,0:T(8,128)(2,1)} %bitcast.132), custom_call_target="tpu_custom_call" | custom-call | flops 4563402752 | bytes 4194304 | tf_op jit(solution)/shard_map/weight_grads/pallas_call | solution.py:600
  220.4 4.3 %all-to-all-start.10 = ((bf16[8,272,128]{2,1,0:T(8,128)(2,1)}), bf16[8,272,128]{2,1,0:T(8,128)(2,1)S(1)}, u32[]{:S(2)}, u32[]{:S(2)}) async-start(bf16[8,272,128]{2,1,0:T(8,128)(2,1)} %get-tuple-element.150), calls=%async_computation.10 | async-start | bytes 1114112 | tf_op jit(solution)/shard_map/all_to_all | solution.py:836
  224.7 10.7 %backward_step.6 = (f32[544,512]{1,0:T(8,128)}, bf16[8,272,128]{2,1,0:T(8,128)(2,1)}, f32[8,128]{1,0:T(8,128)}, f32[32,8,128]{2,1,0:T(8,128)}) custom-call(f32[560,512]{1,0:T(8,128)} %get-tuple-element.135.dz_hbm, f32[32,8,128]{2,1,0:T(8,128)} %copy-done.11, f32[624,512]{1,0:T(8,128)} %get-tuple-element.112.prev_hbm.a_hbm, ...), custom_call_target="tpu_custom_call" | custom-call | flops 4848615424 | bytes 11141120 | tf_op jit(solution)/shard_map/backward_step/pallas_call | solution.py:600
  235.4 6.1 %all-to-all-start.11 = ((f32[32,8,128]{2,1,0:T(8,128)}), f32[32,8,128]{2,1,0:T(8,128)S(1)}, u32[]{:S(2)}, u32[]{:S(2)}) async-start(f32[32,8,128]{2,1,0:T(8,128)} %get-tuple-element.151), calls=%async_computation.11 | async-start | bytes 262144 | tf_op jit(solution)/shard_map/all_to_all | solution.py:661
  241.6 9.9 %weight_grads.6 = bf16[4,17,16,512]{3,2,1,0:T(8,128)(2,1)} custom-call(bf16[8,272,128]{2,1,0:T(8,128)(2,1)} %copy-done.8, bf16[8,528,128]{2,1,0:T(8,128)(2,1)} %chunk_segments.1.segs_ref, bf16[8,512,512]{2,1,0:T(8,128)(2,1)} %bitcast.131), custom_call_target="tpu_custom_call" | custom-call | flops 4563402752 | bytes 4194304 | tf_op jit(solution)/shard_map/weight_grads/pallas_call | solution.py:600
  252.7 3.6 all-to-all-start.12
  257.5 10.4 %backward_step.7 = (f32[528,512]{1,0:T(8,128)}, bf16[8,272,128]{2,1,0:T(8,128)(2,1)}, f32[8,128]{1,0:T(8,128)}, f32[32,8,128]{2,1,0:T(8,128)}) custom-call(f32[544,512]{1,0:T(8,128)} %get-tuple-element.147.dz_hbm, f32[32,8,128]{2,1,0:T(8,128)} %copy-done.9, f32[640,512]{1,0:T(8,128)} %get-tuple-element.110.prev_hbm.a_hbm, ...), custom_call_target="tpu_custom_call" | custom-call | flops 4706009088 | bytes 11075584 | tf_op jit(solution)/shard_map/backward_step/pallas_call | solution.py:600
  268.7 9.8 %weight_grads.7 = bf16[4,17,16,512]{3,2,1,0:T(8,128)(2,1)} custom-call(bf16[8,272,128]{2,1,0:T(8,128)(2,1)} %copy-done.7, bf16[8,528,128]{2,1,0:T(8,128)(2,1)} %chunk_segments.1.segs_ref, bf16[8,512,512]{2,1,0:T(8,128)(2,1)} %bitcast.130), custom_call_target="tpu_custom_call" | custom-call | flops 4563402752 | bytes 4194304 | tf_op jit(solution)/shard_map/weight_grads/pallas_call | solution.py:600
  278.6 5.1 %all-to-all-start.13 = ((f32[32,8,128]{2,1,0:T(8,128)}), f32[32,8,128]{2,1,0:T(8,128)S(1)}, u32[]{:S(2)}, u32[]{:S(2)}) async-start(f32[32,8,128]{2,1,0:T(8,128)} %get-tuple-element.162), calls=%async_computation.13 | async-start | bytes 262144 | tf_op jit(solution)/shard_map/all_to_all | solution.py:661
  284.5 7.8 %all-to-all-done.13.bst_hbm = f32[32,8,128]{2,1,0:T(8,128)S(1)} async-done(((f32[32,8,128]{2,1,0:T(8,128)}), f32[32,8,128]{2,1,0:T(8,128)S(1)}, u32[]{:S(2)}, u32[]{:S(2)}) %all-to-all-start.13) | async-done | bytes 131104 | tf_op jit(solution)/shard_map/all_to_all | solution.py:661
  293.0 4.0 %backward_norm.1 = (bf16[528,512]{1,0:T(8,128)(2,1)}, bf16[8,272,128]{2,1,0:T(8,128)(2,1)}, f32[8,128]{1,0:T(8,128)}) custom-call(f32[528,512]{1,0:T(8,128)} %get-tuple-element.156.dz_hbm, f32[32,8,128]{2,1,0:T(8,128)} %copy-done.12, f32[656,512]{1,0:T(8,128)} %get-tuple-element.105.prev_hbm.a_hbm, f32[32,8,128]{2,1,0:T(8,128)} %copy-done.1, f32[5,512]{1,0:T(8,128)} %gain_hbm.17), custom_call_target="tpu_custom_call" | custom-call | flops 1000 | bytes 4194304 | tf_op jit(solution)/shard_map/backward_norm/pallas_call | solution.py:600
  297.0 3.5 all-to-all-start.14
  305.0 5.1 %all-to-all-done.14.x_ref = bf16[8,272,128]{2,1,0:T(8,128)(2,1)S(1)} async-done(((bf16[8,272,128]{2,1,0:T(8,128)(2,1)}), bf16[8,272,128]{2,1,0:T(8,128)(2,1)S(1)}, u32[]{:S(2)}, u32[]{:S(2)}) %all-to-all-start.14) | async-done | bytes 557088 | tf_op jit(solution)/shard_map/all_to_all | solution.py:836
  310.1 3.5 all-to-all-start.15
  314.0 9.8 %weight_grads.8 = bf16[4,17,16,512]{3,2,1,0:T(8,128)(2,1)} custom-call(bf16[8,272,128]{2,1,0:T(8,128)(2,1)} %copy-done.4, bf16[8,528,128]{2,1,0:T(8,128)(2,1)} %chunk_segments.1.segs_ref, bf16[8,512,512]{2,1,0:T(8,128)(2,1)} %bitcast.129), custom_call_target="tpu_custom_call" | custom-call | flops 4563402752 | bytes 4194304 | tf_op jit(solution)/shard_map/weight_grads/pallas_call | solution.py:600
  325.8 9.7 %weight_grads.9 = bf16[4,17,16,384]{3,2,1,0:T(8,128)(2,1)} custom-call(bf16[8,272,128]{2,1,0:T(8,128)(2,1)} %copy-done.5, bf16[8,528,128]{2,1,0:T(8,128)(2,1)} %chunk_segments.1.segs_ref, bf16[8,512,384]{2,1,0:T(8,128)(2,1)} %all-gather.10.cloned.1.call-done.h_ref), custom_call_target="tpu_custom_call" | custom-call | flops 3422552064 | bytes 3145728 | tf_op jit(solution)/shard_map/weight_grads/pallas_call | solution.py:600
  338.3 9.9 %backward_conv.1 = bf16[512,384]{1,0:T(8,128)(2,1)} custom-call(bf16[528,512]{1,0:T(8,128)(2,1)} %get-tuple-element.173.da_hbm, f32[672,128]{1,0:T(8,128)} %get-tuple-element.104.seg_hbm, bf16[17,512,384]{2,1,0:T(8,128)(2,1)} %bitcast.128, f32[512,384]{1,0:T(8,128)} %get-tuple-element.174.add_hbm), custom_call_target="tpu_custom_call" | custom-call | flops 3422552064 | bytes 8781824 | tf_op jit(solution)/shard_map/backward_conv/pallas_call | solution.py:600
  349.0 3.5 collective-permute-done.16
  353.8 3.1 collective-permute-done.7
  357.0 3.6 reduce-scatter.7.cloned.1.call-done
  364.2 8.4 %collective-permute-done.8 = bf16[17,16,384]{2,1,0:T(8,128)(2,1)S(1)} collective-permute-done((bf16[17,16,384]{2,1,0:T(8,128)(2,1)S(1)}, bf16[17,16,384]{2,1,0:T(8,128)(2,1)S(1)}, u32[]{:S(2)}, u32[]{:S(2)}) %collective-permute-start.8) | collective-permute-done | bytes 208928 | tf_op jit(solution)/shard_map/ppermute | solution.py:658
  376.4 3.4 collective-permute-done.10
  (152 shorter events, 44.5 us)
Async XLA Ops:
  7.2 110.7 %all-gather.10.cloned.1.call-start = ((), (), s32[]{:S(2)}) async-start(), calls=%async_computation.20 | async-start | bytes 3538944 | tf_op jit(solution)/shard_map/all_gather | solution.py:741
  10.2 7.1 %collective-permute-start = (bf16[80,384]{1,0:T(8,128)(2,1)}, bf16[80,384]{1,0:T(8,128)(2,1)S(1)}, u32[]{:S(2)}, u32[]{:S(2)}) collective-permute-start(bf16[80,384]{1,0:T(8,128)(2,1)} %get-tuple-element.102), channel_id=1, source_target_pairs={{0,2},{2,4},{4,6},{6,8},{8,10},{10,12},{12,14},{14,16},{16,18},{18... | collective-permute-start | bytes 184328 | tf_op jit(solution)/shard_map/ppermute | solution.py:684
  12.6 5.5 %collective-permute-start.1 = (bf16[80,384]{1,0:T(8,128)(2,1)}, bf16[80,384]{1,0:T(8,128)(2,1)S(1)}, u32[]{:S(2)}, u32[]{:S(2)}) collective-permute-start(bf16[80,384]{1,0:T(8,128)(2,1)} %get-tuple-element.103), channel_id=1, source_target_pairs={{2,0},{4,2},{6,4},{8,6},{10,8},{12,10},{14,12},{16,14},{18,16},{20... | collective-permute-start | bytes 184328 | tf_op jit(solution)/shard_map/ppermute | solution.py:684
  18.1 19.1 %collective-permute-start.2 = (s32[1,16]{1,0:T(1,128)}, s32[1,16]{1,0:T(1,128)S(1)}, u32[]{:S(2)}, u32[]{:S(2)}) collective-permute-start(s32[1,16]{1,0:T(1,128)} %counts_ref.1), channel_id=1, source_target_pairs={{0,1},{1,0},{2,3},{3,2},{4,5},{5,4},{6,7},{7,6},{8,9},{9,8},{10,11... | collective-permute-start | bytes 200 | tf_op jit(solution)/shard_map/ppermute | solution.py:658
  19.7 17.5 %copy-start.25 = (s32[1,16]{1,0:T(1,128)S(1)}, s32[1,16]{1,0:T(1,128)}, u32[]{:S(2)}) copy-start(s32[1,16]{1,0:T(1,128)} %counts_ref.1) | copy-start | bytes 196
  29.5 16.1 %all-to-all-start = ((f32[32,8,128]{2,1,0:T(8,128)}), f32[32,8,128]{2,1,0:T(8,128)S(1)}, u32[]{:S(2)}, u32[]{:S(2)}) async-start(f32[32,8,128]{2,1,0:T(8,128)} %get-tuple-element.106), calls=%async_computation | async-start | bytes 262144 | tf_op jit(solution)/shard_map/all_to_all | solution.py:661
  37.0 104.9 %all-gather.12.cloned.1.call-start = ((), (), s32[]{:S(2)}) async-start(), calls=%async_computation.25 | async-start | bytes 4718592 | tf_op jit(solution)/shard_map/all_gather | solution.py:741
  70.3 93.2 %all-gather.14.cloned.1.call-start = ((), (), s32[]{:S(2)}) async-start(), calls=%async_computation.26 | async-start | bytes 4718592 | tf_op jit(solution)/shard_map/all_gather | solution.py:741
  104.6 13.3 %all-to-all-start.3 = ((f32[32,16,128]{2,1,0:T(8,128)}), f32[32,16,128]{2,1,0:T(8,128)S(1)}, u32[]{:S(2)}, u32[]{:S(2)}) async-start(f32[32,16,128]{2,1,0:T(8,128)} %get-tuple-element.115), calls=%async_computation.3 | async-start | bytes 524288 | tf_op jit(solution)/shard_map/all_to_all | solution.py:661
  107.2 103.4 %all-gather.16.cloned.1.call-start = ((), (), s32[]{:S(2)}) async-start(), calls=%async_computation.27 | async-start | bytes 4718592 | tf_op jit(solution)/shard_map/all_gather | solution.py:741
  107.2 3.3 collective-permute-start.3
  109.3 4.4 %collective-permute-start.4 = (bf16[48,1024]{1,0:T(8,128)(2,1)S(1)}, bf16[48,1024]{1,0:T(8,128)(2,1)S(1)}, u32[]{:S(2)}, u32[]{:S(2)}) collective-permute-start(bf16[48,1024]{1,0:T(8,128)(2,1)S(1)} %copy-done.27), channel_id=1, source_target_pairs={{2,0},{4,2},{6,4},{8,6},{10,8},{12,10},{14,12},{16,14},{18,16},{20... | collective-permute-start | bytes 294920 | tf_op jit(solution)/shard_map/ppermute | solution.py:754
  110.6 17.6 %copy-start.16 = (bf16[48,1024]{1,0:T(8,128)(2,1)}, bf16[48,1024]{1,0:T(8,128)(2,1)S(1)}, u32[]{:S(2)}) copy-start(bf16[48,1024]{1,0:T(8,128)(2,1)S(1)} %collective-permute-done.3.sl_hbm) | copy-start | bytes 294916
  141.3 100.3 %all-gather.18.cloned.1.call-start = ((), (), s32[]{:S(2)}) async-start(), calls=%async_computation.28 | async-start | bytes 4718592 | tf_op jit(solution)/shard_map/all_gather | solution.py:741
  160.9 13.6 %all-to-all-start.7 = ((f32[32,16,128]{2,1,0:T(8,128)}), f32[32,16,128]{2,1,0:T(8,128)S(1)}, u32[]{:S(2)}, u32[]{:S(2)}) async-start(f32[32,16,128]{2,1,0:T(8,128)} %get-tuple-element.131), calls=%async_computation.7 | async-start | bytes 524288 | tf_op jit(solution)/shard_map/all_to_all | solution.py:661
  174.5 14.5 %all-to-all-start.6 = ((f32[32,8,128]{2,1,0:T(8,128)}), f32[32,8,128]{2,1,0:T(8,128)S(1)}, u32[]{:S(2)}, u32[]{:S(2)}) async-start(f32[32,8,128]{2,1,0:T(8,128)} %get-tuple-element.130), calls=%async_computation.6 | async-start | bytes 262144 | tf_op jit(solution)/shard_map/all_to_all | solution.py:661
  189.0 18.9 %all-to-all-start.8 = ((bf16[8,272,128]{2,1,0:T(8,128)(2,1)}), bf16[8,272,128]{2,1,0:T(8,128)(2,1)S(1)}, u32[]{:S(2)}, u32[]{:S(2)}) async-start(bf16[8,272,128]{2,1,0:T(8,128)(2,1)} %get-tuple-element.138), calls=%async_computation.8 | async-start | bytes 1114112 | tf_op jit(solution)/shard_map/all_to_all | solution.py:836
  193.9 14.1 %collective-permute-start.5 = (bf16[8,1,32,896]{3,2,0,1:T(8,128)(2,1)S(1)}, bf16[8,1,32,896]{3,2,0,1:T(8,128)(2,1)S(1)}, u32[]{:S(2)}, u32[]{:S(2)}) collective-permute-start(bf16[8,1,32,896]{3,2,0,1:T(8,128)(2,1)S(1)} %dynamic-slice_bitcast_fusion), channel_id=1, source_target_pairs={{0,2},{2,0},{4,6},{6,4},{8,10},{10,8},{12,14},{14,12},{16,18},{18,... | collective-permute-start | bytes 1376264 | tf_op jit(solution)/shard_map/ppermute | solution.py:658
  207.9 12.5 %all-to-all-start.9 = ((f32[32,8,128]{2,1,0:T(8,128)}), f32[32,8,128]{2,1,0:T(8,128)S(1)}, u32[]{:S(2)}, u32[]{:S(2)}) async-start(f32[32,8,128]{2,1,0:T(8,128)} %get-tuple-element.142), calls=%async_computation.9 | async-start | bytes 262144 | tf_op jit(solution)/shard_map/all_to_all | solution.py:661
  210.5 81.9 %reduce-scatter.5.cloned.1.call-start = ((), (), s32[]{:S(2)}) async-start(), calls=%async_computation.21 | async-start | bytes 1392640 | tf_op jit(solution)/shard_map/reduce_scatter | solution.py:868
  220.4 15.0 %all-to-all-start.10 = ((bf16[8,272,128]{2,1,0:T(8,128)(2,1)}), bf16[8,272,128]{2,1,0:T(8,128)(2,1)S(1)}, u32[]{:S(2)}, u32[]{:S(2)}) async-start(bf16[8,272,128]{2,1,0:T(8,128)(2,1)} %get-tuple-element.150), calls=%async_computation.10 | async-start | bytes 1114112 | tf_op jit(solution)/shard_map/all_to_all | solution.py:836
  235.4 17.2 %all-to-all-start.11 = ((f32[32,8,128]{2,1,0:T(8,128)}), f32[32,8,128]{2,1,0:T(8,128)S(1)}, u32[]{:S(2)}, u32[]{:S(2)}) async-start(f32[32,8,128]{2,1,0:T(8,128)} %get-tuple-element.151), calls=%async_computation.11 | async-start | bytes 262144 | tf_op jit(solution)/shard_map/all_to_all | solution.py:661
  241.6 82.3 %reduce-scatter.11.cloned.1.call-start = ((), (), s32[]{:S(2)}) async-start(), calls=%async_computation.24 | async-start | bytes 1392640 | tf_op jit(solution)/shard_map/reduce_scatter | solution.py:868
  241.6 14.8 %copy-start.2 = (bf16[512,896]{1,0:T(8,128)(2,1)S(1)}, bf16[512,896]{1,0:T(8,128)(2,1)}, u32[]{:S(2)}) copy-start(bf16[512,896]{1,0:T(8,128)(2,1)} %get-tuple-element.141) | copy-start | bytes 2752516
  252.7 15.2 %all-to-all-start.12 = ((bf16[8,272,128]{2,1,0:T(8,128)(2,1)}), bf16[8,272,128]{2,1,0:T(8,128)(2,1)S(1)}, u32[]{:S(2)}, u32[]{:S(2)}) async-start(bf16[8,272,128]{2,1,0:T(8,128)(2,1)} %get-tuple-element.159), calls=%async_computation.12 | async-start | bytes 1114112 | tf_op jit(solution)/shard_map/all_to_all | solution.py:836
  256.3 96.9 %reduce-scatter.9.cloned.1.call-start = ((), (), s32[]{:S(2)}) async-start(), calls=%async_computation.23 | async-start | bytes 1392640 | tf_op jit(solution)/shard_map/reduce_scatter | solution.py:868
  256.7 11.3 %collective-permute-start.6 = (bf16[2,2,32,896]{3,2,1,0:T(8,128)(2,1)S(1)}, bf16[2,2,32,896]{3,2,1,0:T(8,128)(2,1)S(1)}, u32[]{:S(2)}, u32[]{:S(2)}) collective-permute-start(bf16[2,2,32,896]{3,2,1,0:T(8,128)(2,1)S(1)} %dynamic-slice_bitcast_fusion.2), channel_id=1, source_target_pairs={{0,8},{2,10},{4,12},{6,14},{8,0},{10,2},{12,4},{14,6},{16,24},{18,... | collective-permute-start | bytes 688136 | tf_op jit(solution)/shard_map/ppermute | solution.py:658
  267.9 15.9 %copy-start.20 = (f32[16,128]{1,0:T(8,128)S(1)}, f32[16,128]{1,0:T(8,128)}, u32[]{:S(2)}) copy-start(f32[16,128]{1,0:T(8,128)} %get-tuple-element.191) | copy-start | bytes 24580
  278.5 24.4 %copy-start.21 = (f32[8,128]{1,0:T(8,128)S(1)}, f32[8,128]{1,0:T(8,128)}, u32[]{:S(2)}) copy-start(f32[8,128]{1,0:T(8,128)} %get-tuple-element.187) | copy-start | bytes 12292
  278.5 24.4 %copy-start.22 = (f32[8,128]{1,0:T(8,128)S(1)}, f32[8,128]{1,0:T(8,128)}, u32[]{:S(2)}) copy-start(f32[8,128]{1,0:T(8,128)} %get-tuple-element.186) | copy-start | bytes 12292
  278.5 24.4 %copy-start.23 = (f32[8,128]{1,0:T(8,128)S(1)}, f32[8,128]{1,0:T(8,128)}, u32[]{:S(2)}) copy-start(f32[8,128]{1,0:T(8,128)} %get-tuple-element.185) | copy-start | bytes 12292
  278.5 24.4 %copy-start.24 = (f32[8,128]{1,0:T(8,128)S(1)}, f32[8,128]{1,0:T(8,128)}, u32[]{:S(2)}) copy-start(f32[8,128]{1,0:T(8,128)} %get-tuple-element.184) | copy-start | bytes 12292
  278.6 13.8 %all-to-all-start.13 = ((f32[32,8,128]{2,1,0:T(8,128)}), f32[32,8,128]{2,1,0:T(8,128)S(1)}, u32[]{:S(2)}, u32[]{:S(2)}) async-start(f32[32,8,128]{2,1,0:T(8,128)} %get-tuple-element.162), calls=%async_computation.13 | async-start | bytes 262144 | tf_op jit(solution)/shard_map/all_to_all | solution.py:661
  297.0 13.1 %all-to-all-start.14 = ((bf16[8,272,128]{2,1,0:T(8,128)(2,1)}), bf16[8,272,128]{2,1,0:T(8,128)(2,1)S(1)}, u32[]{:S(2)}, u32[]{:S(2)}) async-start(bf16[8,272,128]{2,1,0:T(8,128)(2,1)} %get-tuple-element.169), calls=%async_computation.15 | async-start | bytes 1114112 | tf_op jit(solution)/shard_map/all_to_all | solution.py:836
  300.5 23.2 %collective-permute-start.13 = (bf16[17,16,512]{2,1,0:T(8,128)(2,1)S(1)}, bf16[17,16,512]{2,1,0:T(8,128)(2,1)S(1)}, u32[]{:S(2)}, u32[]{:S(2)}) collective-permute-start(bf16[17,16,512]{2,1,0:T(8,128)(2,1)S(1)} %bitcast.118), channel_id=1, source_target_pairs={{0,1},{1,0},{2,3},{3,2},{4,5},{5,4},{6,7},{7,6},{8,9},{9,8},{10,11... | collective-permute-start | bytes 835592 | tf_op jit(solution)/shard_map/ppermute | solution.py:658
  302.5 34.1 %collective-permute-start.14 = (bf16[1,2,32,896]{3,2,1,0:T(8,128)(2,1)S(1)}, bf16[1,2,32,896]{3,2,1,0:T(8,128)(2,1)S(1)}, u32[]{:S(2)}, u32[]{:S(2)}) collective-permute-start(bf16[1,2,32,896]{3,2,1,0:T(8,128)(2,1)S(1)} %constant_dynamic-slice_fusion.3), channel_id=1, source_target_pairs={{0,16},{2,18},{4,20},{6,22},{8,24},{10,26},{12,28},{14,30},{16,0},... | collective-permute-start | bytes 344072 | tf_op jit(solution)/shard_map/ppermute | solution.py:658
  310.1 13.7 %all-to-all-start.15 = ((bf16[8,272,128]{2,1,0:T(8,128)(2,1)}), bf16[8,272,128]{2,1,0:T(8,128)(2,1)S(1)}, u32[]{:S(2)}, u32[]{:S(2)}) async-start(bf16[8,272,128]{2,1,0:T(8,128)(2,1)} %get-tuple-element.170), calls=%async_computation.16 | async-start | bytes 1114112 | tf_op jit(solution)/shard_map/all_to_all | solution.py:836
  313.6 47.0 %reduce-scatter.7.cloned.1.call-start = ((), (), s32[]{:S(2)}) async-start(), calls=%async_computation.22 | async-start | bytes 1392640 | tf_op jit(solution)/shard_map/reduce_scatter | solution.py:868
  314.0 66.9 %copy-start.26 = (f32[32]{0:T(128)}, f32[32]{0:T(128)S(1)}, u32[]{:S(2)}) copy-start(f32[32]{0:T(128)S(1)} %fusion.6) | copy-start | bytes 388
  323.9 25.1 %collective-permute-start.12 = (bf16[17,16,512]{2,1,0:T(8,128)(2,1)}, bf16[17,16,512]{2,1,0:T(8,128)(2,1)S(1)}, u32[]{:S(2)}, u32[]{:S(2)}) collective-permute-start(bf16[17,16,512]{2,1,0:T(8,128)(2,1)} %bitcast.117), channel_id=1, source_target_pairs={{0,1},{1,0},{2,3},{3,2},{4,5},{5,4},{6,7},{7,6},{8,9},{9,8},{10,11... | collective-permute-start | bytes 835592 | tf_op jit(solution)/shard_map/ppermute | solution.py:658
  336.6 20.3 %collective-permute-start.7 = (bf16[2,17,16,384]{3,2,1,0:T(8,128)(2,1)S(1)}, bf16[2,17,16,384]{3,2,1,0:T(8,128)(2,1)S(1)}, u32[]{:S(2)}, u32[]{:S(2)}) collective-permute-start(bf16[2,17,16,384]{3,2,1,0:T(8,128)(2,1)S(1)} %dynamic-slice_bitcast_fusion.1), channel_id=1, source_target_pairs={{0,8},{2,10},{4,12},{6,14},{8,0},{10,2},{12,4},{14,6},{16,24},{18,... | collective-permute-start | bytes 1253384 | tf_op jit(solution)/shard_map/ppermute | solution.py:658
  336.7 11.5 %collective-permute-start.15 = (bf16[1,1,32,896]{3,2,1,0:T(8,128)(2,1)S(1)}, bf16[1,1,32,896]{3,2,1,0:T(8,128)(2,1)S(1)}, u32[]{:S(2)}, u32[]{:S(2)}) collective-permute-start(bf16[1,1,32,896]{3,2,1,0:T(8,128)(2,1)S(1)} %constant_dynamic-slice_fusion.2), channel_id=1, source_target_pairs={{0,4},{2,6},{4,0},{6,2},{8,12},{10,14},{12,8},{14,10},{16,20},{18,... | collective-permute-start | bytes 172040 | tf_op jit(solution)/shard_map/ppermute | solution.py:658
  338.3 18.6 %copy-start.3 = (bf16[4,17,16,384]{3,2,1,0:T(8,128)(2,1)S(1)}, bf16[4,17,16,384]{3,2,1,0:T(8,128)(2,1)}, u32[]{:S(2)}) copy-start(bf16[4,17,16,384]{3,2,1,0:T(8,128)(2,1)} %weight_grads.9) | copy-start | bytes 2506756
  348.2 4.2 %collective-permute-start.16 = (bf16[32,896]{1,0:T(8,128)(2,1)S(1)}, bf16[32,896]{1,0:T(8,128)(2,1)S(1)}, u32[]{:S(2)}, u32[]{:S(2)}) collective-permute-start(bf16[32,896]{1,0:T(8,128)(2,1)S(1)} %fusion.4), channel_id=1, source_target_pairs={{0,1},{1,0},{2,3},{3,2},{4,5},{5,4},{6,7},{7,6},{8,9},{9,8},{10,11... | collective-permute-start | bytes 172040 | tf_op jit(solution)/shard_map/ppermute | solution.py:658
  353.1 10.1 %collective-permute-start.11 = (bf16[17,16,512]{2,1,0:T(8,128)(2,1)}, bf16[17,16,512]{2,1,0:T(8,128)(2,1)S(1)}, u32[]{:S(2)}, u32[]{:S(2)}) collective-permute-start(bf16[17,16,512]{2,1,0:T(8,128)(2,1)} %bitcast.119), channel_id=1, source_target_pairs={{0,1},{1,0},{2,3},{3,2},{4,5},{5,4},{6,7},{7,6},{8,9},{9,8},{10,11... | collective-permute-start | bytes 835592 | tf_op jit(solution)/shard_map/ppermute | solution.py:658
  360.6 12.0 %collective-permute-start.9 = (bf16[17,16,512]{2,1,0:T(8,128)(2,1)}, bf16[17,16,512]{2,1,0:T(8,128)(2,1)S(1)}, u32[]{:S(2)}, u32[]{:S(2)}) collective-permute-start(bf16[17,16,512]{2,1,0:T(8,128)(2,1)} %bitcast.120), channel_id=1, source_target_pairs={{0,1},{1,0},{2,3},{3,2},{4,5},{5,4},{6,7},{7,6},{8,9},{9,8},{10,11... | collective-permute-start | bytes 835592 | tf_op jit(solution)/shard_map/ppermute | solution.py:658
  362.1 10.5 %collective-permute-start.8 = (bf16[17,16,384]{2,1,0:T(8,128)(2,1)S(1)}, bf16[17,16,384]{2,1,0:T(8,128)(2,1)S(1)}, u32[]{:S(2)}, u32[]{:S(2)}) collective-permute-start(bf16[17,16,384]{2,1,0:T(8,128)(2,1)S(1)} %dynamic-slice_bitcast_fusion.3), channel_id=1, source_target_pairs={{0,16},{2,18},{4,20},{6,22},{8,24},{10,26},{12,28},{14,30},{16,0},... | collective-permute-start | bytes 626696 | tf_op jit(solution)/shard_map/ppermute | solution.py:658
  372.6 7.2 %collective-permute-start.10 = (bf16[17,16,384]{2,1,0:T(8,128)(2,1)S(1)}, bf16[17,16,384]{2,1,0:T(8,128)(2,1)S(1)}, u32[]{:S(2)}, u32[]{:S(2)}) collective-permute-start(bf16[17,16,384]{2,1,0:T(8,128)(2,1)S(1)} %fusion.3), channel_id=1, source_target_pairs={{0,1},{1,0},{2,3},{3,2},{4,5},{5,4},{6,7},{7,6},{8,9},{9,8},{10,11... | collective-permute-start | bytes 626696 | tf_op jit(solution)/shard_map/ppermute | solution.py:658
  (19 other events, 102.5 us)
Sparse Core Ops, SparseCore 0:
  9.9 36.3 all-gather.9
  70.4 34.6 all-gather.11
  107.6 37.9 all-gather.13
  147.4 37.0 all-gather.15
  186.2 40.4 all-gather.17
  228.9 30.3 reduce-scatter.4
  261.7 26.8 reduce-scatter.10
  290.9 29.6 reduce-scatter.8
  323.9 36.6 reduce-scatter.6
